TPU v7x, 512 devices: a whole 4x8x8 slice. The times are simulated.
512 devices in a mesh: gx: 32 (over x_lo, y, core), gy: 16 (over z, x_hi).
Axes of the slice: x: 4 (x_hi: 2, x_lo: 2; x = x_hi * 2 + x_lo), y: 8, z: 8, core: 2. Of those that a mesh axis runs over, the one named last changes fastest.
Arguments:
- density: float32 [8192, 8192], P('gx', 'gy'), may hold values from 0.05 to 0.95
- kernel_hat: float32 [8192, 8192], P(('gx', 'gy')), may hold values from -18 to 18
Outputs:
- potential: float32 [8192, 8192], P('gx', 'gy')
- new_density: float32 [8192, 8192], P('gx', 'gy')
All inputs are finite; a program needn't handle non-finite values.
Results may differ from a plain program's by a relative error of at most 0.00012.
Values sent between devices are 32-bit elements; how exact they have to be, the bound alone decides.
A program may use at most 64 MiB of HBM per device.

v0:
```python
import math

import jax
import jax.numpy as jnp
from jax import lax
from jax.sharding import PartitionSpec as P

time_step = 0.2
diffusion_rate = 0.25


def padded_2(x, sides, width):
    for axis, dim in sides:
        size, length = (lax.axis_size(axis), x.shape[dim])
        up = [(i, (i + 1) % size) for i in range(size)]
        down = [(j, i) for i, j in up]
        last = lax.slice_in_dim(x, length - width, length, axis=dim)
        leading = lax.slice_in_dim(x, 0, width, axis=dim)
        before = lax.ppermute(last, axis, up)
        after = lax.ppermute(leading, axis, down)
        x = jnp.concatenate([before, x, after], axis=dim)
    return x


def face_flux(lower_rho, upper_rho, lower_pot, upper_pot):
    speed = lower_pot - upper_pot
    drift = jnp.maximum(speed, 0.0) * lower_rho * (1.0 - upper_rho) + jnp.minimum(
        speed, 0.0
    ) * upper_rho * (1.0 - lower_rho)
    spread = diffusion_rate * (lower_rho * lower_rho - upper_rho * upper_rho)
    return drift + spread


def angle_table(count_one, count_two, modulus, exponent_sign):
    first_index = jnp.arange(count_one, dtype=jnp.int32)[:, None]
    second_index = jnp.arange(count_two, dtype=jnp.int32)[None, :]
    product = first_index * second_index % modulus
    angles = exponent_sign * 2.0 * math.pi * product.astype(jnp.float32) / modulus
    return (jnp.cos(angles), jnp.sin(angles))


def highest(form, left_array, right_array):
    return jnp.einsum(form, left_array, right_array, precision=lax.Precision.HIGHEST)


def transform_last(real_part, imag_part, exponent_sign, real_only):
    row_count, length = real_part.shape
    bit_count = length.bit_length() - 1
    outer_len = 1 << bit_count // 2
    inner_len = length // outer_len
    outer_cos, outer_sin = angle_table(outer_len, outer_len, outer_len, exponent_sign)
    shaped_real = real_part.reshape(row_count, outer_len, inner_len)
    section_real = highest("kn,bnm->bkm", outer_cos, shaped_real)
    section_imag = highest("kn,bnm->bkm", outer_sin, shaped_real)
    if imag_part is not None:
        shaped_imag = imag_part.reshape(row_count, outer_len, inner_len)
        section_real = section_real - highest("kn,bnm->bkm", outer_sin, shaped_imag)
        section_imag = section_imag + highest("kn,bnm->bkm", outer_cos, shaped_imag)
    twist_cos, twist_sin = angle_table(outer_len, inner_len, length, exponent_sign)
    turned_real = section_real * twist_cos - section_imag * twist_sin
    turned_imag = section_real * twist_sin + section_imag * twist_cos
    inner_cos, inner_sin = angle_table(inner_len, inner_len, inner_len, exponent_sign)
    out_real = highest("bkn,nm->bkm", turned_real, inner_cos) - highest(
        "bkn,nm->bkm", turned_imag, inner_sin
    )
    result_real = jnp.swapaxes(out_real, 1, 2).reshape(row_count, length)
    if real_only:
        return (result_real, None)
    out_imag = highest("bkn,nm->bkm", turned_real, inner_sin) + highest(
        "bkn,nm->bkm", turned_imag, inner_cos
    )
    result_imag = jnp.swapaxes(out_imag, 1, 2).reshape(row_count, length)
    return (result_real, result_imag)


def local(density, kernel_hat):
    lines_first = lax.all_to_all(density.T, "gx", split_axis=0, concat_axis=1, tiled=True)
    first_real, first_imag = transform_last(lines_first, None, -1.0, False)
    back_real, back_imag = (
        lax.all_to_all(first_real, "gx", split_axis=1, concat_axis=0, tiled=True),
        lax.all_to_all(first_imag, "gx", split_axis=1, concat_axis=0, tiled=True),
    )
    lines_real, lines_imag = (
        lax.all_to_all(back_real.T, "gy", split_axis=0, concat_axis=1, tiled=True),
        lax.all_to_all(back_imag.T, "gy", split_axis=0, concat_axis=1, tiled=True),
    )
    spec_real, spec_imag = transform_last(lines_real, lines_imag, -1.0, False)
    inverse_real, inverse_imag = transform_last(
        spec_real * kernel_hat, spec_imag * kernel_hat, 1.0, False
    )
    block_real, block_imag = (
        lax.all_to_all(inverse_real, "gy", split_axis=1, concat_axis=0, tiled=True),
        lax.all_to_all(inverse_imag, "gy", split_axis=1, concat_axis=0, tiled=True),
    )
    again_real, again_imag = (
        lax.all_to_all(block_real.T, "gx", split_axis=0, concat_axis=1, tiled=True),
        lax.all_to_all(block_imag.T, "gx", split_axis=0, concat_axis=1, tiled=True),
    )
    pot_lines, unused = transform_last(again_real, again_imag, 1.0, True)
    scale = 1.0 / (pot_lines.shape[1] * lines_real.shape[1])
    pot_lines = pot_lines * scale
    potential = lax.all_to_all(pot_lines, "gx", split_axis=1, concat_axis=0, tiled=True).T
    padded = padded_2(jnp.stack([density, potential]), (("gx", 1), ("gy", 2)), 1)
    padded_rho = padded[0]
    padded_pot = padded[1]
    flux_first = face_flux(
        padded_rho[:-1, 1:-1], padded_rho[1:, 1:-1], padded_pot[:-1, 1:-1], padded_pot[1:, 1:-1]
    )
    flux_second = face_flux(
        padded_rho[1:-1, :-1], padded_rho[1:-1, 1:], padded_pot[1:-1, :-1], padded_pot[1:-1, 1:]
    )
    div_first = flux_first[1:] - flux_first[:-1]
    div_second = flux_second[:, 1:] - flux_second[:, :-1]
    new_density = density - time_step * (div_first + div_second)
    return (potential, new_density)


def solution(mesh):
    placed = (P("gx", "gy"), P(("gx", "gy"), None))
    return jax.shard_map(
        local, mesh=mesh, in_specs=placed, out_specs=(P("gx", "gy"), P("gx", "gy")), check_vma=False
    )
```

profile of v0, /device:TPU:1, one launch (start us, length us, event | category | flops | bytes accessed | tf_op | source)
XLA Modules:
  0.0 303.8 jit_solution(4924824498162473648)
XLA Ops:
  0.6 2.0 copy.31
  2.7 10.4 %all-to-all-start = ((f32[32,16,256]{2,1,0:T(8,128)}), f32[32,16,256]{2,1,0:T(8,128)S(1)}, u32[]{:S(2)}, u32[]{:S(2)}) async-start(f32[32,16,256]{2,1,0:T(8,128)} %bitcast.2), calls=%async_computation | async-start | bytes 1048576 | tf_op jit(solution)/shard_map/all_to_all | solution.py:77
  13.2 16.6 %all-to-all-done = f32[32,16,256]{2,1,0:T(8,128)S(1)} async-done(((f32[32,16,256]{2,1,0:T(8,128)}), f32[32,16,256]{2,1,0:T(8,128)S(1)}, u32[]{:S(2)}, u32[]{:S(2)}) %all-to-all-start) | async-done | bytes 524320 | tf_op jit(solution)/shard_map/all_to_all | solution.py:77
  35.0 5.6 %all-to-all-start.1 = ((f32[16,32,256]{2,0,1:T(8,128)}), f32[16,32,256]{2,0,1:T(8,128)S(1)}, u32[]{:S(2)}, u32[]{:S(2)}) async-start(f32[16,32,256]{2,0,1:T(8,128)} %copy.34), calls=%async_computation.1 | async-start | bytes 1048576 | tf_op jit(solution)/shard_map/all_to_all | solution.py:80
  44.1 13.3 %all-to-all-done.1 = f32[16,32,256]{2,0,1:T(8,128)S(1)} async-done(((f32[16,32,256]{2,0,1:T(8,128)}), f32[16,32,256]{2,0,1:T(8,128)S(1)}, u32[]{:S(2)}, u32[]{:S(2)}) %all-to-all-start.1) | async-done | bytes 524320 | tf_op jit(solution)/shard_map/all_to_all | solution.py:80
  57.4 5.6 %all-to-all-start.3 = ((f32[16,32,256]{2,0,1:T(8,128)}), f32[16,32,256]{2,0,1:T(8,128)S(1)}, u32[]{:S(2)}, u32[]{:S(2)}) async-start(f32[16,32,256]{2,0,1:T(8,128)} %copy.38), calls=%async_computation.3 | async-start | bytes 1048576 | tf_op jit(solution)/shard_map/all_to_all | solution.py:81
  64.0 15.7 %all-to-all-done.3 = f32[16,32,256]{2,0,1:T(8,128)S(1)} async-done(((f32[16,32,256]{2,0,1:T(8,128)}), f32[16,32,256]{2,0,1:T(8,128)S(1)}, u32[]{:S(2)}, u32[]{:S(2)}) %all-to-all-start.3) | async-done | bytes 524320 | tf_op jit(solution)/shard_map/all_to_all | solution.py:81
  79.7 11.4 %all-to-all-start.2 = ((f32[16,16,512]{2,1,0:T(8,128)}), f32[16,16,512]{2,1,0:T(8,128)S(1)}, u32[]{:S(2)}, u32[]{:S(2)}) async-start(f32[16,16,512]{2,1,0:T(8,128)} %bitcast.13), calls=%async_computation.2 | async-start | bytes 1048576 | tf_op jit(solution)/shard_map/all_to_all | solution.py:84
  92.2 14.5 %all-to-all-done.2 = f32[16,16,512]{2,1,0:T(8,128)S(1)} async-done(((f32[16,16,512]{2,1,0:T(8,128)}), f32[16,16,512]{2,1,0:T(8,128)S(1)}, u32[]{:S(2)}, u32[]{:S(2)}) %all-to-all-start.2) | async-done | bytes 524320 | tf_op jit(solution)/shard_map/all_to_all | solution.py:84
  106.7 4.9 %all-to-all-start.4 = ((f32[16,16,512]{2,1,0:T(8,128)}), f32[16,16,512]{2,1,0:T(8,128)S(1)}, u32[]{:S(2)}, u32[]{:S(2)}) async-start(f32[16,16,512]{2,1,0:T(8,128)} %bitcast.19), calls=%async_computation.4 | async-start | bytes 1048576 | tf_op jit(solution)/shard_map/all_to_all | solution.py:85
  113.5 12.5 %all-to-all-done.4 = f32[16,16,512]{2,1,0:T(8,128)S(1)} async-done(((f32[16,16,512]{2,1,0:T(8,128)}), f32[16,16,512]{2,1,0:T(8,128)S(1)}, u32[]{:S(2)}, u32[]{:S(2)}) %all-to-all-start.4) | async-done | bytes 524320 | tf_op jit(solution)/shard_map/all_to_all | solution.py:85
  129.6 1.6 fusion.8
  131.2 1.4 copy.42
  138.1 12.2 %fusion.38 = f32[16,64,128]{2,1,0:T(8,128)S(1)} fusion(f32[16,64,128]{2,1,0:T(8,128)S(1)} %fusion.6, f32[16,64,128]{2,1,0:T(8,128)S(1)} %fusion.7, f32[64,128]{1,0:T(8,128)S(1)} %get-tuple-element.16, f32[64,128]{1,0:T(8,128)S(1)} %get-tuple-element.17), kind=kOutput, calls=%fused_computation.71 | convolution fusion | flops 201949184 | bytes 1638400 | tf_op jit(solution)/shard_map/bkn,nm->bkm/dot_general | solution.py:43
  152.8 4.3 %all-to-all-start.5 = ((f32[16,16,512]{2,0,1:T(8,128)}), f32[16,16,512]{2,0,1:T(8,128)S(1)}, u32[]{:S(2)}, u32[]{:S(2)}) async-start(f32[16,16,512]{2,0,1:T(8,128)} %copy.44), calls=%async_computation.5 | async-start | bytes 1048576 | tf_op jit(solution)/shard_map/all_to_all | solution.py:92
  160.5 10.0 %all-to-all-done.5 = f32[16,16,512]{2,0,1:T(8,128)S(1)} async-done(((f32[16,16,512]{2,0,1:T(8,128)}), f32[16,16,512]{2,0,1:T(8,128)S(1)}, u32[]{:S(2)}, u32[]{:S(2)}) %all-to-all-start.5) | async-done | bytes 524320 | tf_op jit(solution)/shard_map/all_to_all | solution.py:92
  170.5 5.0 %all-to-all-start.7 = ((f32[16,16,512]{2,0,1:T(8,128)}), f32[16,16,512]{2,0,1:T(8,128)S(1)}, u32[]{:S(2)}, u32[]{:S(2)}) async-start(f32[16,16,512]{2,0,1:T(8,128)} %copy.48), calls=%async_computation.7 | async-start | bytes 1048576 | tf_op jit(solution)/shard_map/all_to_all | solution.py:93
  176.6 12.4 %all-to-all-done.7 = f32[16,16,512]{2,0,1:T(8,128)S(1)} async-done(((f32[16,16,512]{2,0,1:T(8,128)}), f32[16,16,512]{2,0,1:T(8,128)S(1)}, u32[]{:S(2)}, u32[]{:S(2)}) %all-to-all-start.7) | async-done | bytes 524320 | tf_op jit(solution)/shard_map/all_to_all | solution.py:93
  189.0 17.1 %all-to-all-start.6 = ((f32[32,16,256]{2,1,0:T(8,128)}), f32[32,16,256]{2,1,0:T(8,128)S(1)}, u32[]{:S(2)}, u32[]{:S(2)}) async-start(f32[32,16,256]{2,1,0:T(8,128)} %bitcast.35), calls=%async_computation.6 | async-start | bytes 1048576 | tf_op jit(solution)/shard_map/all_to_all | solution.py:96
  207.1 15.6 %all-to-all-done.6 = f32[32,16,256]{2,1,0:T(8,128)S(1)} async-done(((f32[32,16,256]{2,1,0:T(8,128)}), f32[32,16,256]{2,1,0:T(8,128)S(1)}, u32[]{:S(2)}, u32[]{:S(2)}) %all-to-all-start.6) | async-done | bytes 524320 | tf_op jit(solution)/shard_map/all_to_all | solution.py:96
  222.7 5.7 %all-to-all-start.8 = ((f32[32,16,256]{2,1,0:T(8,128)}), f32[32,16,256]{2,1,0:T(8,128)S(1)}, u32[]{:S(2)}, u32[]{:S(2)}) async-start(f32[32,16,256]{2,1,0:T(8,128)} %bitcast.41), calls=%async_computation.8 | async-start | bytes 1048576 | tf_op jit(solution)/shard_map/all_to_all | solution.py:97
  230.2 14.9 %all-to-all-done.8 = f32[32,16,256]{2,1,0:T(8,128)S(1)} async-done(((f32[32,16,256]{2,1,0:T(8,128)}), f32[32,16,256]{2,1,0:T(8,128)S(1)}, u32[]{:S(2)}, u32[]{:S(2)}) %all-to-all-start.8) | async-done | bytes 524320 | tf_op jit(solution)/shard_map/all_to_all | solution.py:97
  249.5 21.4 %all_to_all.172 = f32[16,32,256]{2,0,1:T(8,128)S(1)} all-to-all(f32[16,32,256]{2,0,1:T(8,128)S(1)} %copy.52), channel_id=1, replica_groups=mesh['gx'=32,'gy'=16] {'gx'}, dimensions={1} | all-to-all | bytes 1048576 | tf_op jit(solution)/shard_map/all_to_all | solution.py:102
  271.0 1.2 fusion.14
  272.2 4.7 %collective-permute-start = (f32[2,1,512]{1,2,0:T(8,128)S(1)}, f32[2,1,512]{1,2,0:T(8,128)S(1)}, u32[]{:S(2)}, u32[]{:S(2)}) collective-permute-start(f32[2,1,512]{1,2,0:T(8,128)S(1)} %get-tuple-element.10), channel_id=1, source_target_pairs={{0,16},{16,32},{32,48},{48,64},{64,80},{80,96},{96,112},{112,128},... | collective-permute-start | bytes 12296 | tf_op jit(solution)/shard_map/ppermute | solution.py:19
  276.9 1.9 collective-permute-start.1
  278.8 4.2 %collective-permute-done = f32[2,1,512]{1,2,0:T(8,128)S(1)} collective-permute-done((f32[2,1,512]{1,2,0:T(8,128)S(1)}, f32[2,1,512]{1,2,0:T(8,128)S(1)}, u32[]{:S(2)}, u32[]{:S(2)}) %collective-permute-start) | collective-permute-done | bytes 4128 | tf_op jit(solution)/shard_map/ppermute | solution.py:19
  283.0 4.4 %collective-permute-done.1 = f32[2,1,512]{1,2,0:T(8,128)S(1)} collective-permute-done((f32[2,1,512]{1,2,0:T(8,128)S(1)}, f32[2,1,512]{1,2,0:T(8,128)S(1)}, u32[]{:S(2)}, u32[]{:S(2)}) %collective-permute-start.1) | collective-permute-done | bytes 4128 | tf_op jit(solution)/shard_map/ppermute | solution.py:20
  288.2 2.5 collective-permute-start.2
  290.7 6.4 %collective-permute-start.3 = (f32[2,258,1]{1,2,0:T(1,128)S(1)}, f32[2,258,1]{1,2,0:T(1,128)S(1)}, u32[]{:S(2)}, u32[]{:S(2)}) collective-permute-start(f32[2,258,1]{1,2,0:T(1,128)S(1)} %get-tuple-element.7), channel_id=1, source_target_pairs={{1,0},{2,1},{3,2},{4,3},{5,4},{6,5},{7,6},{8,7},{9,8},{10,9},{11,1... | collective-permute-start | bytes 6200 | tf_op jit(solution)/shard_map/ppermute | solution.py:20
  298.1 1.7 pad_maximum_fusion
  301.3 1.3 fusion.17
  (73 shorter events, 40.0 us)
Async XLA Ops:
  2.7 27.2 %all-to-all-start = ((f32[32,16,256]{2,1,0:T(8,128)}), f32[32,16,256]{2,1,0:T(8,128)S(1)}, u32[]{:S(2)}, u32[]{:S(2)}) async-start(f32[32,16,256]{2,1,0:T(8,128)} %bitcast.2), calls=%async_computation | async-start | bytes 1048576 | tf_op jit(solution)/shard_map/all_to_all | solution.py:77
  35.0 22.4 %all-to-all-start.1 = ((f32[16,32,256]{2,0,1:T(8,128)}), f32[16,32,256]{2,0,1:T(8,128)S(1)}, u32[]{:S(2)}, u32[]{:S(2)}) async-start(f32[16,32,256]{2,0,1:T(8,128)} %copy.34), calls=%async_computation.1 | async-start | bytes 1048576 | tf_op jit(solution)/shard_map/all_to_all | solution.py:80
  57.4 22.4 %all-to-all-start.3 = ((f32[16,32,256]{2,0,1:T(8,128)}), f32[16,32,256]{2,0,1:T(8,128)S(1)}, u32[]{:S(2)}, u32[]{:S(2)}) async-start(f32[16,32,256]{2,0,1:T(8,128)} %copy.38), calls=%async_computation.3 | async-start | bytes 1048576 | tf_op jit(solution)/shard_map/all_to_all | solution.py:81
  79.7 26.9 %all-to-all-start.2 = ((f32[16,16,512]{2,1,0:T(8,128)}), f32[16,16,512]{2,1,0:T(8,128)S(1)}, u32[]{:S(2)}, u32[]{:S(2)}) async-start(f32[16,16,512]{2,1,0:T(8,128)} %bitcast.13), calls=%async_computation.2 | async-start | bytes 1048576 | tf_op jit(solution)/shard_map/all_to_all | solution.py:84
  106.7 19.4 %all-to-all-start.4 = ((f32[16,16,512]{2,1,0:T(8,128)}), f32[16,16,512]{2,1,0:T(8,128)S(1)}, u32[]{:S(2)}, u32[]{:S(2)}) async-start(f32[16,16,512]{2,1,0:T(8,128)} %bitcast.19), calls=%async_computation.4 | async-start | bytes 1048576 | tf_op jit(solution)/shard_map/all_to_all | solution.py:85
  133.8 1.0 copy-start
  152.8 17.7 %all-to-all-start.5 = ((f32[16,16,512]{2,0,1:T(8,128)}), f32[16,16,512]{2,0,1:T(8,128)S(1)}, u32[]{:S(2)}, u32[]{:S(2)}) async-start(f32[16,16,512]{2,0,1:T(8,128)} %copy.44), calls=%async_computation.5 | async-start | bytes 1048576 | tf_op jit(solution)/shard_map/all_to_all | solution.py:92
  170.5 18.4 %all-to-all-start.7 = ((f32[16,16,512]{2,0,1:T(8,128)}), f32[16,16,512]{2,0,1:T(8,128)S(1)}, u32[]{:S(2)}, u32[]{:S(2)}) async-start(f32[16,16,512]{2,0,1:T(8,128)} %copy.48), calls=%async_computation.7 | async-start | bytes 1048576 | tf_op jit(solution)/shard_map/all_to_all | solution.py:93
  189.0 33.7 %all-to-all-start.6 = ((f32[32,16,256]{2,1,0:T(8,128)}), f32[32,16,256]{2,1,0:T(8,128)S(1)}, u32[]{:S(2)}, u32[]{:S(2)}) async-start(f32[32,16,256]{2,1,0:T(8,128)} %bitcast.35), calls=%async_computation.6 | async-start | bytes 1048576 | tf_op jit(solution)/shard_map/all_to_all | solution.py:96
  222.7 22.4 %all-to-all-start.8 = ((f32[32,16,256]{2,1,0:T(8,128)}), f32[32,16,256]{2,1,0:T(8,128)S(1)}, u32[]{:S(2)}, u32[]{:S(2)}) async-start(f32[32,16,256]{2,1,0:T(8,128)} %bitcast.41), calls=%async_computation.8 | async-start | bytes 1048576 | tf_op jit(solution)/shard_map/all_to_all | solution.py:97
  272.2 10.8 %collective-permute-start = (f32[2,1,512]{1,2,0:T(8,128)S(1)}, f32[2,1,512]{1,2,0:T(8,128)S(1)}, u32[]{:S(2)}, u32[]{:S(2)}) collective-permute-start(f32[2,1,512]{1,2,0:T(8,128)S(1)} %get-tuple-element.10), channel_id=1, source_target_pairs={{0,16},{16,32},{32,48},{48,64},{64,80},{80,96},{96,112},{112,128},... | collective-permute-start | bytes 12296 | tf_op jit(solution)/shard_map/ppermute | solution.py:19
  276.9 10.5 %collective-permute-start.1 = (f32[2,1,512]{1,2,0:T(8,128)S(1)}, f32[2,1,512]{1,2,0:T(8,128)S(1)}, u32[]{:S(2)}, u32[]{:S(2)}) collective-permute-start(f32[2,1,512]{1,2,0:T(8,128)S(1)} %get-tuple-element.11), channel_id=1, source_target_pairs={{16,0},{32,16},{48,32},{64,48},{80,64},{96,80},{112,96},{128,112},... | collective-permute-start | bytes 12296 | tf_op jit(solution)/shard_map/ppermute | solution.py:20
  288.2 9.9 %collective-permute-start.2 = (f32[2,258,1]{1,2,0:T(1,128)S(1)}, f32[2,258,1]{1,2,0:T(1,128)S(1)}, u32[]{:S(2)}, u32[]{:S(2)}) collective-permute-start(f32[2,258,1]{1,2,0:T(1,128)S(1)} %get-tuple-element.6), channel_id=1, source_target_pairs={{0,1},{1,2},{2,3},{3,4},{4,5},{5,6},{6,7},{7,8},{8,9},{9,10},{10,1... | collective-permute-start | bytes 6200 | tf_op jit(solution)/shard_map/ppermute | solution.py:19
  290.7 7.4 %collective-permute-start.3 = (f32[2,258,1]{1,2,0:T(1,128)S(1)}, f32[2,258,1]{1,2,0:T(1,128)S(1)}, u32[]{:S(2)}, u32[]{:S(2)}) collective-permute-start(f32[2,258,1]{1,2,0:T(1,128)S(1)} %get-tuple-element.7), channel_id=1, source_target_pairs={{1,0},{2,1},{3,2},{4,3},{5,4},{6,5},{7,6},{8,7},{9,8},{10,9},{11,1... | collective-permute-start | bytes 6200 | tf_op jit(solution)/shard_map/ppermute | solution.py:20
where the time goes:
time: 306 us; the launch traced here: 304 us
  waiting for transfers between devices  134 us (44%)
  starting transfers between devices  85.6 us (28%)
  matrix products  33.9 us (11%)
  blocking collectives  21.4 us (7%)
  local copies, waits for them, and re-layouts  20.7 us (7%)
  other arithmetic  6.74 us (2%)
    dot_general x28, matrix products, highest(): jnp.einsum(form, left_array, right_array, precision=lax.Precision.HIGHEST)  33.9 us
    all_to_all x1, blocking collectives, local(): lax.all_to_all(pot_lines, 'gx', split_axis=1, concat_axis=0, tiled=True)  21.4 us
    all_to_all x1, starting transfers between devices, local(): lax.all_to_all(block_real.T, 'gx', split_axis=0, concat_axis=1, tiled=True)  17.1 us
    all_to_all x1, waiting for transfers between devices, local(): lax.all_to_all(density.T, 'gx', split_axis=0, concat_axis=1, tiled=True)  16.6 us
    all_to_all x1, waiting for transfers between devices, local(): lax.all_to_all(first_imag, 'gx', split_axis=1, concat_axis=0, tiled=True)  15.7 us
    all_to_all x1, waiting for transfers between devices, local(): lax.all_to_all(block_real.T, 'gx', split_axis=0, concat_axis=1, tiled=True)  15.6 us
    all_to_all x1, waiting for transfers between devices, local(): lax.all_to_all(block_imag.T, 'gx', split_axis=0, concat_axis=1, tiled=True)  14.9 us
    all_to_all x1, waiting for transfers between devices, local(): lax.all_to_all(back_real.T, 'gy', split_axis=0, concat_axis=1, tiled=True)  14.5 us
  transfers between devices with their start and end apart: 13, of which 11 were waited for; matrix products, arithmetic and copies ran while one was open for 5% of the time, Pallas kernels for 0%

commit v1 on v0

v1 whole, which is shorter than its diff:
```python
import functools

import jax
import jax.numpy as jnp
import numpy as np
from jax import lax
from jax.experimental import pallas as pl
from jax.experimental.pallas import tpu as pltpu
from jax.sharding import PartitionSpec as P

TIME_STEP = 0.2
DIFFUSION = 0.25
MESH = pl.DeviceIdType.MESH
F32, BF16 = jnp.float32, jnp.bfloat16
NGX, NGY, N = 32, 16, 8192
ROWS, COLS = 256, 512


def split_np(table):
    table = np.asarray(table, np.float32)
    high = table.astype(BF16)
    low = (table - high.astype(np.float32)).astype(BF16)
    return high, low


def angle(a, b, modulus):
    product = np.asarray(a, np.int64) * np.asarray(b, np.int64) % modulus
    return 2.0 * np.pi * product / modulus


def slot_frequency(half, side, j):
    if half == 0:
        return j + 1 if side == 0 else 16 - j
    return j if side == 0 else 15 - j


@functools.lru_cache(maxsize=None)
def tables():
    t = {}
    eye8 = np.eye(8)
    g = np.arange(32)
    slots = np.arange(16)
    real_rows = np.cos(angle(slots[:, None], g[None], 32))
    imag_rows = -np.sin(angle(slots[:, None], g[None], 32))
    imag_rows[0] = np.cos(angle(16, g, 32))
    t["first"] = split_np(np.kron(np.concatenate([real_rows, imag_rows]), eye8))
    m = np.arange(256)
    theta = angle(slots[:, None], m[None], N)
    last = angle(16, m, N)
    ca, sa, cb, sb = np.cos(theta), np.sin(theta), np.cos(theta), np.sin(theta)
    ca[0], sa[0], cb[0], sb[0] = 0.0, np.cos(last), -np.sin(last), 0.0
    t["twist_first"] = np.repeat(np.stack([ca, sa, cb, sb]), 8, axis=1).astype(np.float32)
    w256 = angle(m[:, None], m[None], 256)
    c256, s256 = np.cos(w256), np.sin(w256)
    forward = np.concatenate([c256, s256], axis=1)
    ones = np.zeros((16, 512))
    ones[0, :256] = 1.0
    t["second"] = split_np(np.concatenate([forward[:128], forward[128:], ones]))
    a = np.arange(512)
    w512 = angle(a[:, None], a[None], 512)
    t["c512"] = split_np(np.cos(w512))
    t["s512"] = split_np(np.sin(w512))
    lane = np.arange(256)
    l16 = 8 * (lane // 128) + lane % 8
    theta = angle(a[:, None], l16[None], N)
    t["twist_rows"] = np.stack([np.cos(theta), np.sin(theta)]).astype(np.float32)
    lin = np.arange(16)
    phi = angle(lin[:, None], lin[None], 16)

    def embed(sign):
        out = np.zeros((2, 2, 8, 8, 2, 16, 8))
        for c in range(2):
            for l8 in range(8):
                co, si = np.cos(phi[8 * c + l8]), sign * np.sin(phi[8 * c + l8])
                for j in range(8):
                    out[c, 0, j, l8, 0, :, j] = co
                    out[c, 0, j, l8, 1, :, j] = si
                    out[c, 1, j, l8, 0, :, j] = -si
                    out[c, 1, j, l8, 1, :, j] = co
        return out.reshape(256, 256)

    def times_i_rows(matrix):
        parts = matrix.reshape(2, 2, 64, -1)
        return np.stack([parts[:, 1], -parts[:, 0]], axis=1).reshape(matrix.shape)

    m2 = embed(-1.0)
    t["sixteen"] = split_np(np.concatenate([m2, times_i_rows(m2)]))
    back = embed(1.0).reshape(2, 2, 8, 8, 2, 16, 8).transpose(4, 5, 6, 0, 1, 2, 3)
    inv = np.zeros((2, 16, 8, 2, 2, 8, 8))
    for c in range(2):
        for l8 in range(8):
            co, si = np.cos(phi[8 * c + l8]), np.sin(phi[8 * c + l8])
            for j in range(8):
                inv[0, :, j, c, 0, j, l8] = co
                inv[0, :, j, c, 1, j, l8] = si
                inv[1, :, j, c, 0, j, l8] = -si
                inv[1, :, j, c, 1, j, l8] = co
    del back
    turned = np.zeros_like(inv)
    turned[:, :, :, :, 0] = -inv[:, :, :, :, 1]
    turned[:, :, :, :, 1] = inv[:, :, :, :, 0]
    t["sixteen_back"] = split_np(np.concatenate([inv.reshape(256, 256), turned.reshape(256, 256)], axis=1))
    t["second_back"] = split_np(
        np.concatenate([np.concatenate([c256[:, h], s256[:, h]]) for h in (slice(0, 128), slice(128, 256))])
    )
    freq = np.zeros((2, 2, 2, 8, 8), np.int64)
    for half in range(2):
        for side in range(2):
            for j in range(8):
                freq[half, side, :, j, :] = slot_frequency(half, side, j)
    flat = freq.reshape(2, 256)
    theta = angle(m[None, :, None], flat[:, None, :], N)
    t["twist_last"] = np.stack([np.cos(theta), np.sin(theta)], axis=1).reshape(4, 256, 256).astype(np.float32)
    last = np.zeros((32, 8, 2, 2, 2, 2, 8, 8))
    scale = 2.0 / (float(N) * float(N))
    for half in range(2):
        for side in range(2):
            conj = 1.0 if side == 0 else -1.0
            for j in range(8):
                arc = angle(g, slot_frequency(half, side, j), 32)
                for l in range(8):
                    last[:, l, half, 0, side, 0, j, l] = scale * np.cos(arc)
                    last[:, l, half, 0, side, 1, j, l] = -scale * np.sin(arc) * conj
                    last[:, l, half, 1, side, 0, j, l] = -scale * np.sin(arc)
                    last[:, l, half, 1, side, 1, j, l] = -scale * np.cos(arc) * conj
    t["last"] = split_np(last.reshape(256, 1024))
    flip = np.zeros((512, 512))
    flip[a, (-a) % 512] = 1.0
    t["flip"] = flip.astype(BF16)
    order = np.zeros((2, 16, 8, 16, 8))
    for kb in range(16):
        for s in range(8):
            order[0, kb, s, kb, 7 - s] = 1.0
            order[1, kb, s, kb, (8 - s) % 8] = 1.0
    t["order"] = order.reshape(2, 128, 128).astype(BF16)
    return t


def split(x):
    high = x.astype(BF16)
    return high, (x - high.astype(F32)).astype(BF16)


def mul(a, b, transposed=False):
    dims = (((1,), (1 if transposed else 0,)), ((), ()))
    dot = lambda x, y: lax.dot_general(x, y, dims, preferred_element_type=F32)
    return dot(a[0], b[0]) + (dot(a[0], b[1]) + dot(a[1], b[0]))


def mul_exact(selector, x, transposed=False):
    dims = (((1,), (1 if transposed else 0,)), ((), ()))
    dot = lambda p, q: lax.dot_general(p, q, dims, preferred_element_type=F32)
    high, low = split(x)
    return dot(selector, high) + dot(selector, low)


def first_forward(x, first, twist, second):
    spun = mul(first, split(x))
    real, imag = spun[:128], spun[128:]
    plain = real[:8]
    turned_real = real * twist[0] + imag * twist[1]
    turned_imag = imag * twist[2] - real * twist[3]

    def rows(table, order):
        return [table[8 * s : 8 * s + 8] for s in order]

    outs = []
    for half in range(2):
        if half == 0:
            near, far = list(range(1, 9)), [0] + list(range(15, 8, -1))
            re, im = turned_real, turned_imag
        else:
            near, far = list(range(8)), list(range(15, 7, -1))
            re = jnp.concatenate([plain, turned_real[8:]], axis=0)
            im = jnp.concatenate([jnp.zeros_like(plain), turned_imag[8:]], axis=0)
        cosine = jnp.concatenate(rows(re, near) + rows(im, near) + rows(re, far) + rows(-im, far), axis=0)
        sine = jnp.concatenate(rows(im, near) + rows(-re, near) + rows(im, far) + rows(re, far), axis=0)
        cosine, sine = split(cosine), split(sine)
        picked = slice(0, 128) if half == 0 else slice(128, 272)
        w = [v[picked] for v in second]
        out = mul([v[:, :256] for v in w], cosine, True) + mul([v[:, 256:] for v in w], sine, True)
        outs.append(out)
    low, high = outs[0], outs[1][:128]
    total = outs[1][128:136, :128]
    tile = high[:8, :128]
    row = lax.broadcasted_iota(jnp.int32, (8, 128), 0)
    lane = lax.broadcasted_iota(jnp.int32, (8, 128), 1)
    tile = jnp.where((row == 0) & (lane >= 64) & (lane < 72), pltpu.roll(tile, 64, 1), tile)
    tile = jnp.where((row == 0) & (lane < 8), total, tile)
    near_high = jnp.concatenate([tile, high[8:, :128]], axis=0)
    return low[:, :128], low[:, 128:], near_high, high[:, 128:]


def first_inverse(low, high, second_back, twist, last):
    row = lax.broadcasted_iota(jnp.int32, (8, 128), 0)
    lane = lax.broadcasted_iota(jnp.int32, (8, 128), 1)
    tile = high[:8, :128]
    constant = jnp.where(lane < 8, 0.5 * tile, 0.0)[:1]
    other = jnp.where(lane < 8, 0.5 * pltpu.roll(tile, 64, 1), jnp.where((lane >= 64) & (lane < 72), 0.0, tile))
    tile = jnp.where(row == 0, other, tile)
    top = jnp.concatenate([tile, high[:8, 128:]], axis=1)
    high = jnp.concatenate([top, high[8:]], axis=0)
    total = None
    for half, x in ((0, low), (1, high)):
        spun = mul([v[512 * half : 512 * half + 512] for v in second_back], split(x))
        cosine, sine = spun[:256], spun[256:]
        if half == 1:
            cosine = jnp.concatenate([cosine[:, :128] + constant, cosine[:, 128:]], axis=1)
        co, si = twist[2 * half], twist[2 * half + 1]
        one = co * cosine - si * sine
        two = si * cosine + co * sine
        for k, part in ((0, one), (1, two)):
            at = 512 * half + 256 * k
            term = mul([v[:, at : at + 256] for v in last], split(part), True)
            total = term if total is None else total + term
    return total


def face_flux(lower_rho, upper_rho, lower_pot, upper_pot):
    speed = lower_pot - upper_pot
    drift = jnp.maximum(speed, 0.0) * lower_rho * (1.0 - upper_rho) + jnp.minimum(speed, 0.0) * upper_rho * (
        1.0 - lower_rho
    )
    return drift + DIFFUSION * (lower_rho * lower_rho - upper_rho * upper_rho)


def weights_layout(own, other, flip, order):
    direct = jnp.concatenate([own[:, 512 * b : 512 * b + 512] for b in range(16)], axis=0)
    mirror = jnp.concatenate([other[:, 512 * (15 - b) : 512 * (15 - b) + 512] for b in range(16)], axis=0)
    turned = mul_exact(flip, mirror, True)
    top = turned[:8]
    row = lax.broadcasted_iota(jnp.int32, (8, 128), 0)
    top = jnp.where(row == 0, pltpu.roll(top, 8, 1), top)
    turned = jnp.concatenate([top, turned[8:]], axis=0)
    high, low = split(turned)
    turned = jnp.dot(high, order, preferred_element_type=F32) + jnp.dot(low, order, preferred_element_type=F32)
    return 0.5 * (direct.T + turned)


CONSTANTS = (
    "first", "twist_first", "second", "c512", "s512", "twist_rows", "sixteen", "sixteen_back",
    "second_back", "twist_last", "last", "flip", "order",
)


def flat_constants():
    out, index = [], {}
    for name in CONSTANTS:
        value = tables()[name]
        value = value if isinstance(value, tuple) else (value,)
        index[name] = list(range(len(out), len(out) + len(value)))
        out.extend(value)
    return out, index


def kernel(index, n_const, *refs):
    rho_ref, kernel_ref = refs[:2]
    const_hbm = refs[2 : 2 + n_const]
    pot_ref, new_ref = refs[2 + n_const : 4 + n_const]
    rest = list(refs[4 + n_const :])
    const = [rest.pop(0) for _ in range(n_const)]
    (
        rho, weights, weights_got, row0_send, row0_got, wk, wk2,
        send1, recv1, send2, recv2, send3, recv3, send4, recv4, send5, recv5, send6, recv6,
        spread, edge_rows, edge_cols, halo_rows, halo_cols, padded_rho, padded_pot,
        send_sem, recv_sem, local_sem, const_sem, k_send, k_recv, halo_send, halo_recv,
    ) = rest
    gx, gy = lax.axis_index("gx"), lax.axis_index("gy")
    device = gx * NGY + gy
    lower = device < 256

    def get(name):
        return [const[i] for i in index[name]]

    mirror = {"gx": NGX - 1 - gx, "gy": NGY - 1 - gy}
    other = jnp.where(device == 0, 256, jnp.where(device == 256, 0, 512 - device))
    row_partner = {"gx": other // NGY, "gy": lax.rem(other, NGY)}

    barrier = pltpu.get_barrier_semaphore()

    def greet(axis, n, me):
        def body(i, carry):
            pl.semaphore_signal(barrier, inc=1, device_id={axis: lax.rem(me + i, n)}, device_id_type=MESH)
            return carry

        lax.fori_loop(1, n, body, 0)

    greet("gx", NGX, gx)
    greet("gy", NGY, gy)
    pl.semaphore_signal(barrier, inc=1, device_id=mirror, device_id_type=MESH)
    pl.semaphore_signal(barrier, inc=1, device_id=row_partner, device_id_type=MESH)

    load_rho = pltpu.make_async_copy(rho_ref, rho, local_sem.at[0])
    load_weights = pltpu.make_async_copy(kernel_ref, weights, local_sem.at[1])
    load_rho.start()
    load_weights.start()
    loads = [pltpu.make_async_copy(const_hbm[i], const[i], const_sem.at[i]) for i in range(n_const)]
    for load in loads:
        load.start()

    def ready(*names):
        for name in names:
            for i in index[name]:
                loads[i].wait()

    load_rho.wait()
    for b in range(4):
        turned = rho[:, 128 * b : 128 * b + 128].T
        for part in range(8):
            for c in range(2):
                send1[c, 8 * b + part] = turned[16 * part + 8 * c : 16 * part + 8 * c + 8]
    edge_rows[0] = rho[0:1, :]
    edge_rows[1] = rho[ROWS - 1 : ROWS, :]
    edge_cols[0] = send1[0, 0, 0:1, :]
    edge_cols[1] = send1[1, NGX - 1, 7:8, :]
    load_weights.wait()
    row0_send[...] = weights[0:1, :]

    pl.semaphore_wait(barrier, NGX - 1 + NGY - 1 + 2)

    def message(phase, c, i, axis, n, me, source, target):
        to = lax.rem(me + i, n)
        return pltpu.make_async_remote_copy(
            src_ref=source(to), dst_ref=target(to), send_sem=send_sem.at[phase, c, i],
            recv_sem=recv_sem.at[phase, c, i], device_id={axis: to}, device_id_type=MESH,
        )

    def start_phase(phase, c, axis, n, me, source, target):
        def body(i, carry):
            message(phase, c, i, axis, n, me, source, target).start()
            return carry

        own = pltpu.make_async_copy(source(me), target(me), local_sem.at[2 + 2 * phase + c])
        own.start()
        lax.fori_loop(1, n, body, 0)

    def finish_phase(phase, c, axis, n, me, source, target):
        def body(i, carry):
            message(phase, c, i, axis, n, me, source, target).wait_recv()
            return carry

        pltpu.make_async_copy(source(me), target(me), local_sem.at[2 + 2 * phase + c]).wait()
        lax.fori_loop(1, n, body, 0)

    def sent_phase(phase, c, axis, n, me, source, target):
        def body(i, carry):
            message(phase, c, i, axis, n, me, source, target).wait_send()
            return carry

        lax.fori_loop(1, n, body, 0)

    def slot_of(y):
        q, b = y // 2, lax.rem(y, 2)
        return b * 8 + jnp.where(b == 0, q, 7 - q)

    def at(ref, c, start, size):
        return ref.at[c, pl.ds(pl.multiple_of(start, size), size)]

    def phase(p, c):
        if p == 0:
            return p, c, "gx", NGX, gx, lambda to: send1.at[c, to], lambda to: recv1.at[c, gx]
        if p == 1:
            return p, c, "gx", NGX, gx, lambda to: at(send2, c, to * 16, 16), lambda to: at(recv2, c, gx * 16, 16)
        if p == 2:
            return (
                p, c, "gy", NGY, gy,
                lambda to: send3.at[c, slot_of(to)],
                lambda to: at(recv3, c, gy * 32, 32),
            )
        if p == 3:
            return (
                p, c, "gy", NGY, gy,
                lambda to: at(send4, c, to * 32, 32),
                lambda to: at(recv4, c, slot_of(gy) * 32, 32),
            )
        if p == 4:
            return p, c, "gx", NGX, gx, lambda to: at(send5, c, to * 16, 16), lambda to: at(recv5, c, gx * 16, 16)
        return (
            p, c, "gx", NGX, gx,
            lambda to: at(send6, c, to * 8, 8),
            lambda to: recv6.at[pl.ds(pl.multiple_of(gx * 16 + 8 * c, 8), 8)],
        )

    def halo(which, kind, source, k):
        axis, n, me = (("gx", NGX, gx), ("gy", NGY, gy))[kind]
        to = lax.rem(me + (n - 1 if k == 0 else 1), n)
        target = halo_rows if kind == 0 else halo_cols
        return pltpu.make_async_remote_copy(
            src_ref=source.at[2 * which + k], dst_ref=target.at[2 * which + k],
            send_sem=halo_send.at[4 * which + 2 * kind + k], recv_sem=halo_recv.at[4 * which + 2 * kind + k],
            device_id={axis: to}, device_id_type=MESH,
        )

    def halos(which):
        return [halo(which, kind, src, k) for kind, src in ((0, edge_rows), (1, edge_cols)) for k in range(2)]

    weights_copy = pltpu.make_async_remote_copy(
        src_ref=weights.at[pl.ds(8, 8)], dst_ref=weights_got, send_sem=k_send.at[0], recv_sem=k_recv.at[0],
        device_id=mirror, device_id_type=MESH,
    )
    row_copy = pltpu.make_async_remote_copy(
        src_ref=row0_send, dst_ref=row0_got, send_sem=k_send.at[1], recv_sem=k_recv.at[1],
        device_id=row_partner, device_id_type=MESH,
    )

    start_phase(*phase(0, 0))
    start_phase(*phase(0, 1))
    weights_copy.start()
    for copy in halos(0):
        copy.start()

    @pl.when(lower)
    def _():
        row_copy.start()

    ready("first", "twist_first", "second")
    first, second, twist_first = get("first"), get("second"), get("twist_first")[0]
    for c in range(2):
        finish_phase(*phase(0, c))
        x = recv1[c].reshape(256, 256)
        near_low, far_low, near_high, far_high = first_forward(
            x, [r[...] for r in first], twist_first, [r[...] for r in second]
        )
        for t in range(16):
            rows = slice(8 * t, 8 * t + 8)
            send2[c, 16 * t : 16 * t + 8] = near_low[rows]
            send2[c, 16 * (16 + t) : 16 * (16 + t) + 8] = near_high[rows]
            send2[c, 16 * (31 - t) + 8 : 16 * (31 - t) + 16] = far_low[rows]
            send2[c, 16 * (15 - t) + 8 : 16 * (15 - t) + 16] = far_high[rows]
        start_phase(*phase(1, c))

    ready("flip", "order")
    flip = get("flip")[0][...]
    order_ref = get("order")[0]
    order = jnp.where(lower, order_ref[0].astype(F32), order_ref[1].astype(F32)).astype(BF16)
    weights_copy.wait_recv()

    @pl.when(jnp.logical_not(lower))
    def _():
        row_copy.wait_recv()
        weights_got[0:1, :] = row0_got[...]

    own = jnp.where(lower, weights[1:9, :], weights[0:8, :])
    spread[...] = own

    @pl.when(device == 256)
    def _():
        one, two = spread[0:1, :], row0_got[...]
        half_difference = 0.5 * (one - two)
        row = lax.broadcasted_iota(jnp.int32, (8, N), 0)
        only = jnp.where(row == 0, jnp.broadcast_to(-half_difference, (8, N)), 0.0)
        wk2[...] = weights_layout(only, only, flip, order)
        half_sum = 0.5 * (one + two)
        spread[0:1, :] = half_sum
        weights_got[0:1, :] = half_sum

    wk[...] = weights_layout(spread[...], weights_got[...], flip, order)

    for c in range(2):
        finish_phase(*phase(1, c))
        for b in range(2):
            for s in range(8):
                send3[c, 8 * b + s] = recv2[c, pl.ds(8 * b + s, 32, stride=16), :]
        start_phase(*phase(2, c))

    ready("c512", "s512", "twist_rows", "sixteen", "sixteen_back")
    c512, s512 = get("c512"), get("s512")
    twist_rows = get("twist_rows")[0]
    sixteen = [r[...] for r in get("sixteen")]
    sixteen_back = [r[...] for r in get("sixteen_back")]
    finish_phase(*phase(2, 0))
    finish_phase(*phase(2, 1))
    x = split(jnp.concatenate([recv3[0], recv3[1]], axis=1))
    lane = lax.broadcasted_iota(jnp.int32, (1, 256), 1)
    sign = jnp.where(lax.rem(lane // 64, 2) == 0, 1.0, -1.0)
    ones_v, twos_v = [], []
    for block in range(4):
        rows = slice(128 * block, 128 * block + 128)
        cosine = mul([r[rows, :] for r in c512], x)
        sine = mul([r[rows, :] for r in s512], x)
        co, si = twist_rows[0, rows, :], twist_rows[1, rows, :]
        one = co * cosine - si * sine
        two = -(si * cosine + co * sine)
        v = split(jnp.concatenate([one, two], axis=1))
        spec = mul(v, sixteen)
        w = wk[rows, :]
        prod_real, prod_imag = spec[:, :128] * w, spec[:, 128:] * w
        send4[0, rows] = prod_real
        send4[1, rows] = prod_imag

        @pl.when(device == 256)
        def _():
            spec2 = mul(split(jnp.concatenate([one * sign, two * sign], axis=1)), sixteen)
            w2 = wk2[rows, :]
            send4[0, rows] = send4[0, rows] + spec2[:, :128] * w2
            send4[1, rows] = send4[1, rows] + spec2[:, 128:] * w2

        prod = split(jnp.concatenate([send4[0, rows], send4[1, rows]], axis=1))
        u = mul(prod, sixteen_back)
        u, ui = u[:, :256], u[:, 256:]
        ones_v.append(u * co + ui * si)
        twos_v.append(ui * co - u * si)
    one = split(jnp.concatenate(ones_v, axis=0))
    two = split(jnp.concatenate(twos_v, axis=0))
    for c in range(2):
        lanes = slice(128 * c, 128 * c + 128)
        one_c, two_c = [v[:, lanes] for v in one], [v[:, lanes] for v in two]
        for block in range(4):
            rows = slice(128 * block, 128 * block + 128)
            send4[c, rows] = mul([r[rows, :] for r in c512], one_c) + mul([r[rows, :] for r in s512], two_c)
        start_phase(*phase(3, c))

    for c in range(2):
        finish_phase(*phase(3, c))
        for g in range(NGX):
            for b in range(2):
                send5[c, 16 * g + 8 * b : 16 * g + 8 * b + 8] = recv4[c, pl.ds(256 * b + g, 8, stride=32), :]
        start_phase(*phase(4, c))

    ready("second_back", "twist_last", "last")
    second_back = [r[...] for r in get("second_back")]
    twist_last = get("twist_last")[0]
    last = [r[...] for r in get("last")]
    for c in range(2):
        finish_phase(*phase(4, c))
        near = [recv5[c, 16 * t : 16 * t + 8] for t in range(32)]
        far = [recv5[c, 16 * (31 - t) + 8 : 16 * (31 - t) + 16] for t in range(32)]
        near, far = jnp.concatenate(near, axis=0), jnp.concatenate(far, axis=0)
        both = jnp.concatenate([near, far], axis=1)
        send6[c] = first_inverse(both[:128], both[128:], second_back, twist_last, last)
        start_phase(*phase(5, c))

    for copy in halos(0):
        copy.wait_recv()
    finish_phase(*phase(5, 0))
    finish_phase(*phase(5, 1))
    for b in range(4):
        padded_pot[8 : 8 + ROWS, 128 * b : 128 * b + 128] = recv6[128 * b : 128 * b + 128, :].T
    edge_rows[2] = padded_pot[8:9, :]
    edge_rows[3] = padded_pot[7 + ROWS : 8 + ROWS, :]
    edge_cols[2] = recv6[0:1, :]
    edge_cols[3] = recv6[COLS - 1 : COLS, :]
    for copy in halos(1):
        copy.start()
    pot_ref[...] = padded_pot[8 : 8 + ROWS, :]
    padded_rho[8 : 8 + ROWS, :] = rho[...]
    padded_rho[7:8, :] = halo_rows[1]
    padded_rho[8 + ROWS : 9 + ROWS, :] = halo_rows[0]
    for copy in halos(1):
        copy.wait_recv()
    padded_pot[7:8, :] = halo_rows[3]
    padded_pot[8 + ROWS : 9 + ROWS, :] = halo_rows[2]
    columns = jnp.concatenate([halo_cols[k] for k in range(4)] + [jnp.zeros((4, ROWS), F32)], axis=0).T
    lane = lax.broadcasted_iota(jnp.int32, (32, COLS), 1)
    for block in range(8):
        base = 8 + 32 * block
        r, p = padded_rho[base : base + 32, :], padded_pot[base : base + 32, :]
        cols = columns[32 * block : 32 * block + 32]
        above = face_flux(r, padded_rho[base + 1 : base + 33, :], p, padded_pot[base + 1 : base + 33, :])
        below = face_flux(padded_rho[base - 1 : base + 31, :], r, padded_pot[base - 1 : base + 31, :], p)
        r_next = jnp.where(lane == COLS - 1, cols[:, 0:1], pltpu.roll(r, COLS - 1, 1))
        p_next = jnp.where(lane == COLS - 1, cols[:, 2:3], pltpu.roll(p, COLS - 1, 1))
        right = face_flux(r, r_next, p, p_next)
        r_edge = jnp.broadcast_to(cols[:, 1:2], (32, 128))
        p_edge = jnp.broadcast_to(cols[:, 3:4], (32, 128))
        first_left = face_flux(r_edge, r[:, :128], p_edge, p[:, :128])[:, 0:1]
        left = jnp.where(lane == 0, first_left, pltpu.roll(right, 1, 1))
        new_ref[32 * block : 32 * block + 32, :] = r - TIME_STEP * ((above - below) + (right - left))

    for p in range(6):
        for c in range(2):
            sent_phase(*phase(p, c))
    for copy in halos(0) + halos(1):
        copy.wait_send()
    weights_copy.wait_send()

    @pl.when(lower)
    def _():
        row_copy.wait_send()


def local(density, kernel_hat):
    constants, index = flat_constants()
    vmem = lambda *shape: pltpu.VMEM(shape, F32)
    n_const = len(constants)
    scratch = [pltpu.VMEM(c.shape, c.dtype) for c in constants] + [
        vmem(ROWS, COLS), vmem(16, N), vmem(8, N), vmem(1, N), vmem(1, N), vmem(512, 128), vmem(512, 128),
        vmem(2, 32, 8, 256), vmem(2, 32, 8, 256),
        vmem(2, 512, 128), vmem(2, 512, 128),
        vmem(2, 16, 32, 128), vmem(2, 512, 128),
        vmem(2, 512, 128), vmem(2, 512, 128),
        vmem(2, 512, 128), vmem(2, 512, 128),
        vmem(2, 256, 256), vmem(512, 256),
        vmem(8, N), vmem(4, 1, COLS), vmem(4, 1, ROWS), vmem(4, 1, COLS), vmem(4, 1, ROWS),
        vmem(ROWS + 16, COLS), vmem(ROWS + 16, COLS),
        pltpu.SemaphoreType.DMA((6, 2, 32)), pltpu.SemaphoreType.DMA((6, 2, 32)),
        pltpu.SemaphoreType.DMA((14,)), pltpu.SemaphoreType.DMA((n_const,)),
        pltpu.SemaphoreType.DMA((2,)), pltpu.SemaphoreType.DMA((2,)),
        pltpu.SemaphoreType.DMA((8,)), pltpu.SemaphoreType.DMA((8,)),
    ]
    out = jax.ShapeDtypeStruct((ROWS, COLS), F32)
    return pl.pallas_call(
        functools.partial(kernel, index, n_const),
        out_shape=(out, out),
        in_specs=[pl.BlockSpec(memory_space=pl.ANY)] * (2 + n_const),
        out_specs=(pl.BlockSpec(memory_space=pltpu.VMEM),) * 2,
        scratch_shapes=scratch,
        compiler_params=pltpu.CompilerParams(
            collective_id=0, has_side_effects=True, vmem_limit_bytes=56 * 1024 * 1024
        ),
        name="convolve_step",
    )(density, kernel_hat, *[jnp.asarray(c) for c in constants])


def solution(mesh):
    return jax.shard_map(
        local, mesh=mesh, in_specs=(P("gx", "gy"), P(("gx", "gy"), None)),
        out_specs=(P("gx", "gy"), P("gx", "gy")), check_vma=False,
    )
```

time: 306 us -> 130 us (0.42)
  waiting for transfers between devices: 134 us -> 0 us
  Pallas kernels: 0 us -> 127 us
  starting transfers between devices: 85.6 us -> 0 us
  matrix products: 33.9 us -> 0 us
  blocking collectives: 21.4 us -> 0 us
  local copies, waits for them, and re-layouts: 20.7 us -> 2.72 us
  other arithmetic: 6.74 us -> 0 us
    pallas_call x0 -> x1, Pallas kernels: none -> 127 us  [local(): pl.pallas_call(functools.partial(kernel, index, n_const), out_shape=(out,...]
    all_to_all x9 -> x0, waiting for transfers between devices: 125 us -> none  [the longest x1 16.6 us: local(): lax.all_to_all(density.T, 'gx', split_axis=0, concat_axis=1, tiled=True)]
    all_to_all x9 -> x0, starting transfers between devices: 70.1 us -> none  [the longest x1 17.1 us: local(): lax.all_to_all(block_real.T, 'gx', split_axis=0, concat_axis=1, tiled=True)]
    dot_general x28 -> x0, matrix products: 33.9 us -> none  [highest(): jnp.einsum(form, left_array, right_array, precision=lax.Precision.HIGHEST)]
    all_to_all x1 -> x0, blocking collectives: 21.4 us -> none  [local(): lax.all_to_all(pot_lines, 'gx', split_axis=1, concat_axis=0, tiled=True)]
    ppermute x4 -> x0, starting transfers between devices: 15.5 us -> none  [the longest x2 8.3 us: padded_2(): after = lax.ppermute(leading, axis, down)]
    ppermute x4 -> x0, waiting for transfers between devices: 8.58 us -> none  [the longest x2 4.4 us: padded_2(): after = lax.ppermute(leading, axis, down)]
    all_to_all x13 -> x0, local copies, waits for them, and re-layouts: 7.1 us -> none  [the longest x2 1.41 us: local(): lax.all_to_all(first_imag, 'gx', split_axis=1, concat_axis=0, tiled=True)]
  transfers between devices with their start and end apart: 13 -> 0, of which waited for: 11 -> 0; matrix products, arithmetic and copies ran while one was open for 5% -> 0% of each run, Pallas kernels for 0% -> 0%
where the time goes in v1:
time: 130 us
  Pallas kernels  127 us (98%)
  local copies, waits for them, and re-layouts  2.72 us (2%)
    pallas_call x1, Pallas kernels, local(): pl.pallas_call(functools.partial(kernel, index, n_const), out_shape=(out,...  127 us
    unnamed x4, local copies, waits for them, and re-layouts  2.72 us

profile of v1, /device:TPU:1, one launch (start us, length us, event | category | flops | bytes accessed | tf_op | source)
XLA Modules:
  0.0 130.2 jit_solution(4011032350020842448)
XLA Ops:
  0.6 126.8 %convolve_step.1 = (f32[256,512]{1,0:T(8,128)}, f32[256,512]{1,0:T(8,128)}) custom-call(f32[256,512]{1,0:T(8,128)} %refs_0_.1, f32[16,8192]{1,0:T(8,128)} %refs_1_.1, bf16[256,256]{1,0:T(8,128)(2,1)} %constant.42.clone.refs_2_, bf16[256,256]{1,0:T(8,128)(2,1)} %constant.43.clone.refs_3_, f32[4,128,256]{2,1,0:T(8,128)} %constant.44.clone.refs_4_, ...), custom_call_target="tpu_custom_call" | custom-call | tf_op jit(solution)/shard_map/convolve_step/pallas_call | solution.py:602
  127.4 0.0 copy-start
  127.4 1.9 %copy.27 = f32[256,512]{1,0:T(8,128)} copy(f32[256,512]{1,0:T(8,128)} %get-tuple-element.4) | data formatting | bytes 1048576
  129.4 0.0 copy-done
  129.4 0.8 copy.28
Async XLA Ops:
  127.4 1.9 %copy-start = (f32[256,512]{1,0:T(8,128)S(1)}, f32[256,512]{1,0:T(8,128)}, u32[]{:S(2)}) copy-start(f32[256,512]{1,0:T(8,128)} %get-tuple-element.5) | copy-start | bytes 1572868

commit v2 on v1

--- a/solution.py
+++ b/solution.py
@@ -84,8 +84,8 @@
         return np.stack([parts[:, 1], -parts[:, 0]], axis=1).reshape(matrix.shape)
 
     m2 = embed(-1.0)
-    t["sixteen"] = split_np(np.concatenate([m2, times_i_rows(m2)]))
-    back = embed(1.0).reshape(2, 2, 8, 8, 2, 16, 8).transpose(4, 5, 6, 0, 1, 2, 3)
+    both = np.stack([m2, times_i_rows(m2)]).reshape(2, 2, 128, 256).transpose(1, 0, 2, 3)
+    t["sixteen"] = split_np(both.reshape(2, 256, 256))
     inv = np.zeros((2, 16, 8, 2, 2, 8, 8))
     for c in range(2):
         for l8 in range(8):
@@ -95,11 +95,11 @@
                 inv[0, :, j, c, 1, j, l8] = si
                 inv[1, :, j, c, 0, j, l8] = -si
                 inv[1, :, j, c, 1, j, l8] = co
-    del back
     turned = np.zeros_like(inv)
     turned[:, :, :, :, 0] = -inv[:, :, :, :, 1]
     turned[:, :, :, :, 1] = inv[:, :, :, :, 0]
-    t["sixteen_back"] = split_np(np.concatenate([inv.reshape(256, 256), turned.reshape(256, 256)], axis=1))
+    both = np.stack([inv.reshape(256, 2, 128), turned.reshape(256, 2, 128)], axis=2)
+    t["sixteen_back"] = split_np(both.transpose(1, 0, 2, 3).reshape(2, 256, 256))
     t["second_back"] = split_np(
         np.concatenate([np.concatenate([c256[:, h], s256[:, h]]) for h in (slice(0, 128), slice(128, 256))])
     )
@@ -224,8 +224,11 @@
     return drift + DIFFUSION * (lower_rho * lower_rho - upper_rho * upper_rho)
 
 
-def weights_layout(own, other, flip, order):
-    direct = jnp.concatenate([own[:, 512 * b : 512 * b + 512] for b in range(16)], axis=0)
+def direct_layout(own):
+    return 0.5 * jnp.concatenate([own[:, 512 * b : 512 * b + 512] for b in range(16)], axis=0).T
+
+
+def mirror_layout(other, flip, order):
     mirror = jnp.concatenate([other[:, 512 * (15 - b) : 512 * (15 - b) + 512] for b in range(16)], axis=0)
     turned = mul_exact(flip, mirror, True)
     top = turned[:8]
@@ -233,8 +236,8 @@
     top = jnp.where(row == 0, pltpu.roll(top, 8, 1), top)
     turned = jnp.concatenate([top, turned[8:]], axis=0)
     high, low = split(turned)
-    turned = jnp.dot(high, order, preferred_element_type=F32) + jnp.dot(low, order, preferred_element_type=F32)
-    return 0.5 * (direct.T + turned)
+    dot = lambda x: jnp.dot(x, order, preferred_element_type=F32)
+    return 0.5 * (dot(high) + dot(low))
 
 
 CONSTANTS = (
@@ -256,25 +259,23 @@
 def kernel(index, n_const, *refs):
     rho_ref, kernel_ref = refs[:2]
     const_hbm = refs[2 : 2 + n_const]
-    pot_ref, new_ref = refs[2 + n_const : 4 + n_const]
+    pot_ref, div_ref = refs[2 + n_const : 4 + n_const]
     rest = list(refs[4 + n_const :])
     const = [rest.pop(0) for _ in range(n_const)]
     (
-        rho, weights, weights_got, row0_send, row0_got, wk, wk2,
+        rho, weights, weights_mid, weights_turned, weights_got, row0_send, row0_mid, row0_got, only, wk, wk2, spec, spec2,
         send1, recv1, send2, recv2, send3, recv3, send4, recv4, send5, recv5, send6, recv6,
-        spread, edge_rows, edge_cols, halo_rows, halo_cols, padded_rho, padded_pot,
-        send_sem, recv_sem, local_sem, const_sem, k_send, k_recv, halo_send, halo_recv,
+        edge_rows, edge_cols, halo_rows, halo_cols, padded_rho, padded_pot, pot_out, div_out,
+        send_sem, recv_sem, local_sem, load_sem, const_sem, k_send, k_recv, halo_send, halo_recv,
     ) = rest
     gx, gy = lax.axis_index("gx"), lax.axis_index("gy")
+    x_low, y_at, core = gx // 16, lax.rem(gx // 2, 8), lax.rem(gx, 2)
+    z_at, x_high = gy // 2, lax.rem(gy, 2)
     device = gx * NGY + gy
-    lower = device < 256
+    lower = gx < NGX // 2
 
     def get(name):
         return [const[i] for i in index[name]]
-
-    mirror = {"gx": NGX - 1 - gx, "gy": NGY - 1 - gy}
-    other = jnp.where(device == 0, 256, jnp.where(device == 256, 0, 512 - device))
-    row_partner = {"gx": other // NGY, "gy": lax.rem(other, NGY)}
 
     barrier = pltpu.get_barrier_semaphore()
 
@@ -287,11 +288,9 @@
 
     greet("gx", NGX, gx)
     greet("gy", NGY, gy)
-    pl.semaphore_signal(barrier, inc=1, device_id=mirror, device_id_type=MESH)
-    pl.semaphore_signal(barrier, inc=1, device_id=row_partner, device_id_type=MESH)
-
-    load_rho = pltpu.make_async_copy(rho_ref, rho, local_sem.at[0])
-    load_weights = pltpu.make_async_copy(kernel_ref, weights, local_sem.at[1])
+
+    load_rho = pltpu.make_async_copy(rho_ref, rho, load_sem.at[0])
+    load_weights = pltpu.make_async_copy(kernel_ref, weights, load_sem.at[1])
     load_rho.start()
     load_weights.start()
     loads = [pltpu.make_async_copy(const_hbm[i], const[i], const_sem.at[i]) for i in range(n_const)]
@@ -316,107 +315,147 @@
     load_weights.wait()
     row0_send[...] = weights[0:1, :]
 
-    pl.semaphore_wait(barrier, NGX - 1 + NGY - 1 + 2)
-
-    def message(phase, c, i, axis, n, me, source, target):
-        to = lax.rem(me + i, n)
-        return pltpu.make_async_remote_copy(
-            src_ref=source(to), dst_ref=target(to), send_sem=send_sem.at[phase, c, i],
-            recv_sem=recv_sem.at[phase, c, i], device_id={axis: to}, device_id_type=MESH,
-        )
-
-    def start_phase(phase, c, axis, n, me, source, target):
-        def body(i, carry):
-            message(phase, c, i, axis, n, me, source, target).start()
-            return carry
-
-        own = pltpu.make_async_copy(source(me), target(me), local_sem.at[2 + 2 * phase + c])
-        own.start()
-        lax.fori_loop(1, n, body, 0)
-
-    def finish_phase(phase, c, axis, n, me, source, target):
-        def body(i, carry):
-            message(phase, c, i, axis, n, me, source, target).wait_recv()
-            return carry
-
-        pltpu.make_async_copy(source(me), target(me), local_sem.at[2 + 2 * phase + c]).wait()
-        lax.fori_loop(1, n, body, 0)
-
-    def sent_phase(phase, c, axis, n, me, source, target):
-        def body(i, carry):
-            message(phase, c, i, axis, n, me, source, target).wait_send()
-            return carry
-
-        lax.fori_loop(1, n, body, 0)
+    @pl.when(lax.rem(gy, 8) == 0)
+    def _():
+        row0_mid[...] = weights[0:1, :]
+
+    pl.semaphore_wait(barrier, NGX - 1 + NGY - 1)
+
+    def far_first(t):
+        return jnp.where(lax.rem(t, 2) == 1, 4 - (t + 1) // 2, 4 + t // 2)
+
+    def peer_gx(i):
+        x = lax.rem(x_low + 1 - i // 16, 2)
+        y = lax.rem(y_at + far_first(lax.rem(i, 16) // 2), 8)
+        return x * 16 + y * 2 + lax.rem(core + 1 - lax.rem(i, 2), 2)
+
+    def peer_gy(i):
+        return lax.rem(z_at + far_first(i // 2), 8) * 2 + lax.rem(x_high + 1 - lax.rem(i, 2), 2)
 
     def slot_of(y):
         q, b = y // 2, lax.rem(y, 2)
         return b * 8 + jnp.where(b == 0, q, 7 - q)
 
-    def at(ref, c, start, size):
-        return ref.at[c, pl.ds(pl.multiple_of(start, size), size)]
-
-    def phase(p, c):
+    def at(ref, where, start, size):
+        return ref.at[(*where, pl.ds(pl.multiple_of(start, 8), size))]
+
+    def ends(p, c, h, to):
+        half = 16 * lax.rem(x_low + 1 - h, 2)
         if p == 0:
-            return p, c, "gx", NGX, gx, lambda to: send1.at[c, to], lambda to: recv1.at[c, gx]
+            return send1.at[c, to], recv1.at[c, gx]
         if p == 1:
-            return p, c, "gx", NGX, gx, lambda to: at(send2, c, to * 16, 16), lambda to: at(recv2, c, gx * 16, 16)
+            return at(send2, (c,), to * 16, 16), at(recv2, (c,), 256 * h + lax.rem(gx, 16) * 16, 16)
         if p == 2:
-            return (
-                p, c, "gy", NGY, gy,
-                lambda to: send3.at[c, slot_of(to)],
-                lambda to: at(recv3, c, gy * 32, 32),
-            )
+            return at(send3, (c,), 256 * h + slot_of(to) * 16, 16), at(recv3, (c,), gy * 32 + half, 16)
         if p == 3:
-            return (
-                p, c, "gy", NGY, gy,
-                lambda to: at(send4, c, to * 32, 32),
-                lambda to: at(recv4, c, slot_of(gy) * 32, 32),
-            )
+            return at(send4, (c,), to * 32 + half, 16), at(recv4, (c,), 256 * h + slot_of(gy) * 16, 16)
         if p == 4:
-            return p, c, "gx", NGX, gx, lambda to: at(send5, c, to * 16, 16), lambda to: at(recv5, c, gx * 16, 16)
-        return (
-            p, c, "gx", NGX, gx,
-            lambda to: at(send6, c, to * 8, 8),
-            lambda to: recv6.at[pl.ds(pl.multiple_of(gx * 16 + 8 * c, 8), 8)],
+            return at(send5, (c,), 256 * h + lax.rem(to, 16) * 16, 16), at(recv5, (c,), gx * 16, 16)
+        return at(send6, (c,), to * 8, 8), recv6.at[pl.ds(pl.multiple_of(gx * 16 + 8 * c, 8), 8)]
+
+    def message(p, c, h, i):
+        over_gy = p in (2, 3)
+        to = peer_gy(i) if over_gy else peer_gx(i + 16 * h)
+        source, target = ends(p, c, h, to)
+        return pltpu.make_async_remote_copy(
+            src_ref=source, dst_ref=target, send_sem=send_sem.at[p, c], recv_sem=recv_sem.at[p, c, h],
+            device_id={"gy" if over_gy else "gx": to}, device_id_type=MESH,
         )
 
-    def halo(which, kind, source, k):
+    def count(p, h):
+        return 16 if p not in (2, 3) and h == 0 else 15
+
+    def own_copy(p, c, h):
+        source, target = ends(p, c, h, gy if p in (2, 3) else gx)
+        return pltpu.make_async_copy(source, target, local_sem.at[p, c, h])
+
+    def start(p, c, h):
+        def body(i, carry):
+            message(p, c, h, i).start()
+            return carry
+
+        if count(p, h) == 15:
+            own_copy(p, c, h).start()
+        lax.fori_loop(0, count(p, h), body, 0)
+
+    def group(some, p, c, h):
+        return pltpu.make_async_remote_copy(
+            src_ref=some, dst_ref=some, send_sem=send_sem.at[p, c], recv_sem=recv_sem.at[p, c, h],
+            device_id={"gx": lax.rem(gx + 1, NGX)}, device_id_type=MESH,
+        )
+
+    def finish(p, c, h):
+        n = count(p, h)
+        if n == 15:
+            own_copy(p, c, h).wait()
+        if p == 0:
+            some = recv1.at[c, pl.ds(0, n)]
+        elif p == 5:
+            some = recv6.at[pl.ds(0, 8 * n)]
+        else:
+            some = (None, recv2, recv3, recv4, recv5)[p].at[c, pl.ds(0, 16 * n)]
+        group(some, p, c, h).wait_recv()
+
+    def sent(p, c):
+        if p == 0:
+            some = send1.at[c, pl.ds(0, 31)]
+        elif p == 5:
+            some = send6.at[c, pl.ds(0, 8 * 31)]
+        else:
+            some = (None, send2, send3, send4, send5)[p].at[c, pl.ds(0, 16 * (30 if p in (2, 3) else 31))]
+        group(some, p, c, 0).wait_send()
+
+    def halo(which, kind, k):
         axis, n, me = (("gx", NGX, gx), ("gy", NGY, gy))[kind]
         to = lax.rem(me + (n - 1 if k == 0 else 1), n)
-        target = halo_rows if kind == 0 else halo_cols
+        source, target = ((edge_rows, halo_rows), (edge_cols, halo_cols))[kind]
         return pltpu.make_async_remote_copy(
             src_ref=source.at[2 * which + k], dst_ref=target.at[2 * which + k],
             send_sem=halo_send.at[4 * which + 2 * kind + k], recv_sem=halo_recv.at[4 * which + 2 * kind + k],
             device_id={axis: to}, device_id_type=MESH,
         )
 
-    def halos(which):
-        return [halo(which, kind, src, k) for kind, src in ((0, edge_rows), (1, edge_cols)) for k in range(2)]
-
-    weights_copy = pltpu.make_async_remote_copy(
-        src_ref=weights.at[pl.ds(8, 8)], dst_ref=weights_got, send_sem=k_send.at[0], recv_sem=k_recv.at[0],
-        device_id=mirror, device_id_type=MESH,
-    )
-    row_copy = pltpu.make_async_remote_copy(
-        src_ref=row0_send, dst_ref=row0_got, send_sem=k_send.at[1], recv_sem=k_recv.at[1],
-        device_id=row_partner, device_id_type=MESH,
-    )
-
-    start_phase(*phase(0, 0))
-    start_phase(*phase(0, 1))
-    weights_copy.start()
-    for copy in halos(0):
-        copy.start()
+    def relay(source, target, k, where):
+        return pltpu.make_async_remote_copy(
+            src_ref=source, dst_ref=target, send_sem=k_send.at[k], recv_sem=k_recv.at[k], device_id=where,
+            device_id_type=MESH,
+        )
+
+    weights_first = relay(weights.at[pl.ds(8, 8)], weights_mid, 0, {"gy": NGY - 1 - gy})
+    weights_second = relay(weights_turned, weights_got, 1, {"gx": NGX - 1 - gx})
+    row_first = relay(row0_send, row0_mid, 2, {"gy": lax.rem(NGY - gy, NGY)})
+    edge_gx = jnp.where(gx == 0, 16, jnp.where(gx == 16, 0, lax.rem(NGX - gx, NGX)))
+    row_second = relay(row0_mid, row0_got, 3, {"gx": jnp.where(gy == 0, edge_gx, NGX - 1 - gx)})
+    row_moves = lower & (lax.rem(gy, 8) != 0)
+
+    for c in range(2):
+        for h in range(2):
+            start(0, c, h)
+    weights_first.start()
+
+    @pl.when(row_moves)
+    def _():
+        row_first.start()
+
+    for kind in range(2):
+        for k in range(2):
+            halo(0, kind, k).start()
+
+    wk[...] = direct_layout(jnp.where(lower, weights[1:9, :], weights[0:8, :]))
+
+    @pl.when(row_moves)
+    def _():
+        row_first.wait_recv()
 
     @pl.when(lower)
     def _():
-        row_copy.start()
+        row_second.start()
 
     ready("first", "twist_first", "second")
     first, second, twist_first = get("first"), get("second"), get("twist_first")[0]
     for c in range(2):
-        finish_phase(*phase(0, c))
+        finish(0, c, 0)
+        finish(0, c, 1)
         x = recv1[c].reshape(256, 256)
         near_low, far_low, near_high, far_high = first_forward(
             x, [r[...] for r in first], twist_first, [r[...] for r in second]
@@ -427,132 +466,149 @@
             send2[c, 16 * (16 + t) : 16 * (16 + t) + 8] = near_high[rows]
             send2[c, 16 * (31 - t) + 8 : 16 * (31 - t) + 16] = far_low[rows]
             send2[c, 16 * (15 - t) + 8 : 16 * (15 - t) + 16] = far_high[rows]
-        start_phase(*phase(1, c))
+        start(1, c, 0)
+        start(1, c, 1)
 
     ready("flip", "order")
     flip = get("flip")[0][...]
     order_ref = get("order")[0]
-    order = jnp.where(lower, order_ref[0].astype(F32), order_ref[1].astype(F32)).astype(BF16)
-    weights_copy.wait_recv()
+    weights_first.wait_recv()
+
+    @pl.when(lower)
+    def _():
+        weights_mid[0:1, :] = jnp.zeros((1, N), F32)
+        weights_turned[...] = mirror_layout(weights_mid[...], flip, order_ref[1])
 
     @pl.when(jnp.logical_not(lower))
     def _():
-        row_copy.wait_recv()
-        weights_got[0:1, :] = row0_got[...]
-
-    own = jnp.where(lower, weights[1:9, :], weights[0:8, :])
-    spread[...] = own
-
-    @pl.when(device == 256)
-    def _():
-        one, two = spread[0:1, :], row0_got[...]
-        half_difference = 0.5 * (one - two)
+        weights_turned[...] = mirror_layout(weights_mid[...], flip, order_ref[0])
+
+    weights_second.start()
+
+    @pl.when(jnp.logical_not(lower))
+    def _():
+        row_second.wait_recv()
         row = lax.broadcasted_iota(jnp.int32, (8, N), 0)
-        only = jnp.where(row == 0, jnp.broadcast_to(-half_difference, (8, N)), 0.0)
-        wk2[...] = weights_layout(only, only, flip, order)
-        half_sum = 0.5 * (one + two)
-        spread[0:1, :] = half_sum
-        weights_got[0:1, :] = half_sum
-
-    wk[...] = weights_layout(spread[...], weights_got[...], flip, order)
-
-    for c in range(2):
-        finish_phase(*phase(1, c))
-        for b in range(2):
-            for s in range(8):
-                send3[c, 8 * b + s] = recv2[c, pl.ds(8 * b + s, 32, stride=16), :]
-        start_phase(*phase(2, c))
+
+        @pl.when(device == 256)
+        def _():
+            one, two = weights[0:1, :], row0_got[...]
+            only[...] = jnp.where(row == 0, jnp.broadcast_to(0.5 * (two - one), (8, N)), 0.0)
+            change = direct_layout(only[...])
+            wk[...] = wk[...] + change
+            wk2[...] = change + mirror_layout(only[...], flip, order_ref[1])
+            row0_got[...] = 0.5 * (one + two)
+
+        only[...] = jnp.where(row == 0, jnp.broadcast_to(row0_got[...], (8, N)), 0.0)
+        wk[...] = wk[...] + mirror_layout(only[...], flip, order_ref[1])
+
+    for c in range(2):
+        for h in range(2):
+            finish(1, c, h)
+            for slot in range(16):
+                rows = slice(256 * h + 16 * slot, 256 * h + 16 * slot + 16)
+                send3[c, rows] = recv2[c, pl.ds(256 * h + slot, 16, stride=16), :]
+            start(2, c, h)
 
     ready("c512", "s512", "twist_rows", "sixteen", "sixteen_back")
-    c512, s512 = get("c512"), get("s512")
-    twist_rows = get("twist_rows")[0]
-    sixteen = [r[...] for r in get("sixteen")]
-    sixteen_back = [r[...] for r in get("sixteen_back")]
-    finish_phase(*phase(2, 0))
-    finish_phase(*phase(2, 1))
-    x = split(jnp.concatenate([recv3[0], recv3[1]], axis=1))
-    lane = lax.broadcasted_iota(jnp.int32, (1, 256), 1)
-    sign = jnp.where(lax.rem(lane // 64, 2) == 0, 1.0, -1.0)
-    ones_v, twos_v = [], []
-    for block in range(4):
-        rows = slice(128 * block, 128 * block + 128)
-        cosine = mul([r[rows, :] for r in c512], x)
-        sine = mul([r[rows, :] for r in s512], x)
-        co, si = twist_rows[0, rows, :], twist_rows[1, rows, :]
+    c512, s512 = [r[...] for r in get("c512")], [r[...] for r in get("s512")]
+    twist_rows, sixteen, sixteen_back = get("twist_rows")[0], get("sixteen"), get("sixteen_back")
+    lane = lax.broadcasted_iota(jnp.int32, (1, 128), 1)
+    sign = jnp.where(lane < 64, 1.0, -1.0)
+    for c in range(2):
+        lanes = slice(128 * c, 128 * c + 128)
+        finish(2, c, 0)
+        finish(2, c, 1)
+        x = split(recv3[c])
+        cosine, sine = mul(c512, x), mul(s512, x)
+        co, si = twist_rows[0, :, lanes], twist_rows[1, :, lanes]
         one = co * cosine - si * sine
         two = -(si * cosine + co * sine)
-        v = split(jnp.concatenate([one, two], axis=1))
-        spec = mul(v, sixteen)
-        w = wk[rows, :]
-        prod_real, prod_imag = spec[:, :128] * w, spec[:, 128:] * w
-        send4[0, rows] = prod_real
-        send4[1, rows] = prod_imag
+        matrix = [r[c] for r in sixteen]
+        part = mul(split(jnp.concatenate([one, two], axis=1)), matrix)
+        spec[...] = part if c == 0 else spec[...] + part
 
         @pl.when(device == 256)
         def _():
-            spec2 = mul(split(jnp.concatenate([one * sign, two * sign], axis=1)), sixteen)
-            w2 = wk2[rows, :]
-            send4[0, rows] = send4[0, rows] + spec2[:, :128] * w2
-            send4[1, rows] = send4[1, rows] + spec2[:, 128:] * w2
-
-        prod = split(jnp.concatenate([send4[0, rows], send4[1, rows]], axis=1))
-        u = mul(prod, sixteen_back)
-        u, ui = u[:, :256], u[:, 256:]
-        ones_v.append(u * co + ui * si)
-        twos_v.append(ui * co - u * si)
-    one = split(jnp.concatenate(ones_v, axis=0))
-    two = split(jnp.concatenate(twos_v, axis=0))
+            part = mul(split(jnp.concatenate([one * sign, two * sign], axis=1)), matrix)
+            spec2[...] = part if c == 0 else spec2[...] + part
+
+    weights_second.wait_recv()
+    both_weights = wk[...] + weights_got[...]
+    spec[:, :128] = spec[:, :128] * both_weights
+    spec[:, 128:] = spec[:, 128:] * both_weights
+
+    @pl.when(device == 256)
+    def _():
+        spec[:, :128] = spec[:, :128] + spec2[:, :128] * wk2[...]
+        spec[:, 128:] = spec[:, 128:] + spec2[:, 128:] * wk2[...]
+
+    prod = split(spec[...])
     for c in range(2):
         lanes = slice(128 * c, 128 * c + 128)
-        one_c, two_c = [v[:, lanes] for v in one], [v[:, lanes] for v in two]
-        for block in range(4):
-            rows = slice(128 * block, 128 * block + 128)
-            send4[c, rows] = mul([r[rows, :] for r in c512], one_c) + mul([r[rows, :] for r in s512], two_c)
-        start_phase(*phase(3, c))
-
-    for c in range(2):
-        finish_phase(*phase(3, c))
-        for g in range(NGX):
-            for b in range(2):
-                send5[c, 16 * g + 8 * b : 16 * g + 8 * b + 8] = recv4[c, pl.ds(256 * b + g, 8, stride=32), :]
-        start_phase(*phase(4, c))
+        u = mul(prod, [r[c] for r in sixteen_back])
+        u, ui = u[:, :128], u[:, 128:]
+        co, si = twist_rows[0, :, lanes], twist_rows[1, :, lanes]
+        send4[c] = mul(c512, split(u * co + ui * si)) + mul(s512, split(ui * co - u * si))
+        start(3, c, 0)
+        start(3, c, 1)
+
+    for c in range(2):
+        for h in range(2):
+            finish(3, c, h)
+            for r in range(16):
+                for b in range(2):
+                    base = 256 * h + 16 * r + 8 * b
+                    send5[c, base : base + 8] = recv4[c, pl.ds(256 * h + 128 * b + r, 8, stride=16), :]
+            start(4, c, h)
 
     ready("second_back", "twist_last", "last")
     second_back = [r[...] for r in get("second_back")]
     twist_last = get("twist_last")[0]
     last = [r[...] for r in get("last")]
     for c in range(2):
-        finish_phase(*phase(4, c))
+        finish(4, c, 0)
+        finish(4, c, 1)
         near = [recv5[c, 16 * t : 16 * t + 8] for t in range(32)]
         far = [recv5[c, 16 * (31 - t) + 8 : 16 * (31 - t) + 16] for t in range(32)]
         near, far = jnp.concatenate(near, axis=0), jnp.concatenate(far, axis=0)
         both = jnp.concatenate([near, far], axis=1)
         send6[c] = first_inverse(both[:128], both[128:], second_back, twist_last, last)
-        start_phase(*phase(5, c))
-
-    for copy in halos(0):
-        copy.wait_recv()
-    finish_phase(*phase(5, 0))
-    finish_phase(*phase(5, 1))
+        start(5, c, 0)
+        start(5, c, 1)
+
+    padded_rho[8 : 8 + ROWS, :] = rho[...]
+    for kind in range(2):
+        for k in range(2):
+            halo(0, kind, k).wait_recv()
+    padded_rho[7:8, :] = halo_rows[1]
+    padded_rho[8 + ROWS : 9 + ROWS, :] = halo_rows[0]
+    for c in range(2):
+        for h in range(2):
+            finish(5, c, h)
+    edge_cols[2] = recv6[0:1, :]
+    edge_cols[3] = recv6[COLS - 1 : COLS, :]
+    for k in range(2):
+        halo(1, 1, k).start()
     for b in range(4):
         padded_pot[8 : 8 + ROWS, 128 * b : 128 * b + 128] = recv6[128 * b : 128 * b + 128, :].T
     edge_rows[2] = padded_pot[8:9, :]
     edge_rows[3] = padded_pot[7 + ROWS : 8 + ROWS, :]
-    edge_cols[2] = recv6[0:1, :]
-    edge_cols[3] = recv6[COLS - 1 : COLS, :]
-    for copy in halos(1):
-        copy.start()
-    pot_ref[...] = padded_pot[8 : 8 + ROWS, :]
-    padded_rho[8 : 8 + ROWS, :] = rho[...]
-    padded_rho[7:8, :] = halo_rows[1]
-    padded_rho[8 + ROWS : 9 + ROWS, :] = halo_rows[0]
-    for copy in halos(1):
-        copy.wait_recv()
-    padded_pot[7:8, :] = halo_rows[3]
-    padded_pot[8 + ROWS : 9 + ROWS, :] = halo_rows[2]
+    for k in range(2):
+        halo(1, 0, k).start()
+    pot_out[...] = 0.5 * padded_pot[8 : 8 + ROWS, :]
+    pot_store = pltpu.make_async_copy(pot_out, pot_ref, load_sem.at[2])
+    pot_store.start()
+    for k in range(2):
+        halo(1, 1, k).wait_recv()
     columns = jnp.concatenate([halo_cols[k] for k in range(4)] + [jnp.zeros((4, ROWS), F32)], axis=0).T
     lane = lax.broadcasted_iota(jnp.int32, (32, COLS), 1)
-    for block in range(8):
+    for block in (1, 2, 3, 4, 5, 6, 0, 7):
+        if block == 0:
+            for k in range(2):
+                halo(1, 0, k).wait_recv()
+            padded_pot[7:8, :] = halo_rows[3]
+            padded_pot[8 + ROWS : 9 + ROWS, :] = halo_rows[2]
         base = 8 + 32 * block
         r, p = padded_rho[base : base + 32, :], padded_pot[base : base + 32, :]
         cols = columns[32 * block : 32 * block + 32]
@@ -565,51 +621,61 @@
         p_edge = jnp.broadcast_to(cols[:, 3:4], (32, 128))
         first_left = face_flux(r_edge, r[:, :128], p_edge, p[:, :128])[:, 0:1]
         left = jnp.where(lane == 0, first_left, pltpu.roll(right, 1, 1))
-        new_ref[32 * block : 32 * block + 32, :] = r - TIME_STEP * ((above - below) + (right - left))
+        div_out[32 * block : 32 * block + 32, :] = (above - below) + (right - left)
+    div_store = pltpu.make_async_copy(div_out, div_ref, load_sem.at[3])
+    div_store.start()
 
     for p in range(6):
         for c in range(2):
-            sent_phase(*phase(p, c))
-    for copy in halos(0) + halos(1):
-        copy.wait_send()
-    weights_copy.wait_send()
+            sent(p, c)
+    for which in range(2):
+        for kind in range(2):
+            for k in range(2):
+                halo(which, kind, k).wait_send()
+    weights_first.wait_send()
+    weights_second.wait_send()
+
+    @pl.when(row_moves)
+    def _():
+        row_first.wait_send()
 
     @pl.when(lower)
     def _():
-        row_copy.wait_send()
+        row_second.wait_send()
+
+    pot_store.wait()
+    div_store.wait()
 
 
 def local(density, kernel_hat):
     constants, index = flat_constants()
     vmem = lambda *shape: pltpu.VMEM(shape, F32)
+    dma = lambda *shape: pltpu.SemaphoreType.DMA(shape)
     n_const = len(constants)
     scratch = [pltpu.VMEM(c.shape, c.dtype) for c in constants] + [
-        vmem(ROWS, COLS), vmem(16, N), vmem(8, N), vmem(1, N), vmem(1, N), vmem(512, 128), vmem(512, 128),
+        vmem(ROWS, COLS), vmem(16, N), vmem(8, N), vmem(512, 128), vmem(512, 128), vmem(1, N), vmem(1, N), vmem(1, N), vmem(8, N),
+        vmem(512, 128), vmem(512, 128), vmem(512, 256), vmem(512, 256),
         vmem(2, 32, 8, 256), vmem(2, 32, 8, 256),
-        vmem(2, 512, 128), vmem(2, 512, 128),
-        vmem(2, 16, 32, 128), vmem(2, 512, 128),
-        vmem(2, 512, 128), vmem(2, 512, 128),
-        vmem(2, 512, 128), vmem(2, 512, 128),
+        vmem(2, 512, 128), vmem(2, 512, 128), vmem(2, 512, 128), vmem(2, 512, 128),
+        vmem(2, 512, 128), vmem(2, 512, 128), vmem(2, 512, 128), vmem(2, 512, 128),
         vmem(2, 256, 256), vmem(512, 256),
-        vmem(8, N), vmem(4, 1, COLS), vmem(4, 1, ROWS), vmem(4, 1, COLS), vmem(4, 1, ROWS),
-        vmem(ROWS + 16, COLS), vmem(ROWS + 16, COLS),
-        pltpu.SemaphoreType.DMA((6, 2, 32)), pltpu.SemaphoreType.DMA((6, 2, 32)),
-        pltpu.SemaphoreType.DMA((14,)), pltpu.SemaphoreType.DMA((n_const,)),
-        pltpu.SemaphoreType.DMA((2,)), pltpu.SemaphoreType.DMA((2,)),
-        pltpu.SemaphoreType.DMA((8,)), pltpu.SemaphoreType.DMA((8,)),
+        vmem(4, 1, COLS), vmem(4, 1, ROWS), vmem(4, 1, COLS), vmem(4, 1, ROWS),
+        vmem(ROWS + 16, COLS), vmem(ROWS + 16, COLS), vmem(ROWS, COLS), vmem(ROWS, COLS),
+        dma(6, 2), dma(6, 2, 2), dma(6, 2, 2), dma(4), dma(n_const), dma(4), dma(4), dma(8), dma(8),
     ]
     out = jax.ShapeDtypeStruct((ROWS, COLS), F32)
-    return pl.pallas_call(
+    half_potential, divergence = pl.pallas_call(
         functools.partial(kernel, index, n_const),
         out_shape=(out, out),
         in_specs=[pl.BlockSpec(memory_space=pl.ANY)] * (2 + n_const),
-        out_specs=(pl.BlockSpec(memory_space=pltpu.VMEM),) * 2,
+        out_specs=(pl.BlockSpec(memory_space=pl.ANY),) * 2,
         scratch_shapes=scratch,
         compiler_params=pltpu.CompilerParams(
             collective_id=0, has_side_effects=True, vmem_limit_bytes=56 * 1024 * 1024
         ),
         name="convolve_step",
     )(density, kernel_hat, *[jnp.asarray(c) for c in constants])
+    return 2.0 * half_potential, density - TIME_STEP * divergence
 
 
 def solution(mesh):

time: 130 us -> 108 us (0.83)
  Pallas kernels: 127 us -> 105 us
  local copies, waits for them, and re-layouts: 2.72 us -> 0.01 us
  other arithmetic: 0 us -> 2.33 us
    pallas_call x1, Pallas kernels: 127 us -> 105 us  [local(): pl.pallas_call(functools.partial(kernel, index, n_const), out_shape=(out,...]
    unnamed x4 -> x2, local copies, waits for them, and re-layouts: 2.72 us -> 0.01 us
    sub x0 -> x1, other arithmetic: none -> 2.33 us  [local(): return (2.0 * half_potential, density - TIME_STEP * divergence)]
where the time goes in v2:
time: 108 us
  Pallas kernels  105 us (97%)
  other arithmetic  2.33 us (2%)
    pallas_call x1, Pallas kernels, local(): pl.pallas_call(functools.partial(kernel, index, n_const), out_shape=(out,...  105 us
    sub x1, other arithmetic, local(): return (2.0 * half_potential, density - TIME_STEP * divergence)  2.33 us

profile of v2, /device:TPU:1, one launch (start us, length us, event | category | flops | bytes accessed | tf_op | source)
XLA Modules:
  0.0 107.7 jit_solution(9499603536513571239)
XLA Ops:
  0.6 0.0 copy-start
  0.6 104.7 %convolve_step.1 = (f32[256,512]{1,0:T(8,128)}, f32[256,512]{1,0:T(8,128)}) custom-call(f32[256,512]{1,0:T(8,128)} %refs_0_.1, f32[16,8192]{1,0:T(8,128)} %refs_1_.1, bf16[256,256]{1,0:T(8,128)(2,1)} %constant.46.clone.refs_2_, bf16[256,256]{1,0:T(8,128)(2,1)} %constant.47.clone.refs_3_, f32[4,128,256]{2,1,0:T(8,128)} %constant.48.clone.refs_4_, ...), custom_call_target="tpu_custom_call" | custom-call | tf_op jit(solution)/shard_map/convolve_step/pallas_call | solution.py:667
  105.4 0.0 copy-done
  105.4 2.3 %multiply_subtract_fusion = (f32[256,512]{1,0:T(8,128)}, f32[256,512]{1,0:T(8,128)}) fusion(f32[256,512]{1,0:T(8,128)S(1)} %copy-done, f32[256,512]{1,0:T(8,128)} %get-tuple-element.5, f32[256,512]{1,0:T(8,128)} %get-tuple-element.4), kind=kLoop, calls=%fused_computation | loop fusion | flops 393216 | bytes 2621440 | tf_op jit(solution)/shard_map/sub | solution.py:678
Async XLA Ops:
  0.6 104.8 %copy-start = (f32[256,512]{1,0:T(8,128)S(1)}, f32[256,512]{1,0:T(8,128)}, u32[]{:S(2)}) copy-start(f32[256,512]{1,0:T(8,128)} %refs_0_.1) | copy-start | bytes 1572868

commit v3 on v2

--- a/solution.py
+++ b/solution.py
@@ -256,16 +256,28 @@
     return out, index
 
 
-def kernel(index, n_const, *refs):
+def pack(values):
+    pieces, stacks = [], ([], [])
+    for i, value in enumerate(values):
+        which = 0 if value.dtype == np.float32 else 1
+        planes = value if value.ndim == 3 else value[None]
+        for k, plane in enumerate(planes):
+            begin = sum(p.shape[0] for p in stacks[which])
+            pieces.append((i, k if value.ndim == 3 else None, which, begin, *plane.shape))
+            stacks[which].append(np.pad(plane, ((0, 0), (0, 1024 - plane.shape[1]))))
+    return pieces, [np.concatenate(stack) for stack in stacks]
+
+
+def kernel(index, n_const, pieces, *refs):
     rho_ref, kernel_ref = refs[:2]
-    const_hbm = refs[2 : 2 + n_const]
-    pot_ref, div_ref = refs[2 + n_const : 4 + n_const]
-    rest = list(refs[4 + n_const :])
+    packs = refs[2:4]
+    pot_ref, new_ref = refs[4:6]
+    rest = list(refs[6:])
     const = [rest.pop(0) for _ in range(n_const)]
     (
         rho, weights, weights_mid, weights_turned, weights_got, row0_send, row0_mid, row0_got, only, wk, wk2, spec, spec2,
         send1, recv1, send2, recv2, send3, recv3, send4, recv4, send5, recv5, send6, recv6,
-        edge_rows, edge_cols, halo_rows, halo_cols, padded_rho, padded_pot, pot_out, div_out,
+        edge_rows, edge_cols, halo_rows, halo_cols, padded_rho, padded_pot, pot_out, new_out,
         send_sem, recv_sem, local_sem, load_sem, const_sem, k_send, k_recv, halo_send, halo_recv,
     ) = rest
     gx, gy = lax.axis_index("gx"), lax.axis_index("gy")
@@ -286,6 +298,8 @@
 
         lax.fori_loop(1, n, body, 0)
 
+    across = {"gx": gx + 16 - 32 * x_low, "gy": NGY - 1 - gy}
+    pl.semaphore_signal(barrier, inc=1, device_id=across, device_id_type=MESH)
     greet("gx", NGX, gx)
     greet("gy", NGY, gy)
 
@@ -293,14 +307,19 @@
     load_weights = pltpu.make_async_copy(kernel_ref, weights, load_sem.at[1])
     load_rho.start()
     load_weights.start()
-    loads = [pltpu.make_async_copy(const_hbm[i], const[i], const_sem.at[i]) for i in range(n_const)]
-    for load in loads:
+    loads = [[] for _ in range(n_const)]
+    for at_piece, (i, k, which, begin, rows, width) in enumerate(pieces):
+        source = packs[which].at[pl.ds(begin, rows), pl.ds(0, width)]
+        target = const[i] if k is None else const[i].at[k]
+        load = pltpu.make_async_copy(source, target, const_sem.at[at_piece])
         load.start()
+        loads[i].append(load)
 
     def ready(*names):
         for name in names:
             for i in index[name]:
-                loads[i].wait()
+                for load in loads[i]:
+                    load.wait()
 
     load_rho.wait()
     for b in range(4):
@@ -319,18 +338,21 @@
     def _():
         row0_mid[...] = weights[0:1, :]
 
-    pl.semaphore_wait(barrier, NGX - 1 + NGY - 1)
+    pl.semaphore_wait(barrier, NGX - 1 + NGY - 1 + 1)
+
+    def wrap(x, n):
+        return jnp.where(x >= n, x - n, x)
 
     def far_first(t):
-        return jnp.where(lax.rem(t, 2) == 1, 4 - (t + 1) // 2, 4 + t // 2)
+        return 4 - (t + 1) // 2 if t % 2 else 4 + t // 2
 
     def peer_gx(i):
-        x = lax.rem(x_low + 1 - i // 16, 2)
-        y = lax.rem(y_at + far_first(lax.rem(i, 16) // 2), 8)
-        return x * 16 + y * 2 + lax.rem(core + 1 - lax.rem(i, 2), 2)
+        x = x_low if i // 16 else 1 - x_low
+        y = wrap(y_at + far_first(i % 16 // 2), 8)
+        return x * 16 + y * 2 + (core if i % 2 else 1 - core)
 
     def peer_gy(i):
-        return lax.rem(z_at + far_first(i // 2), 8) * 2 + lax.rem(x_high + 1 - lax.rem(i, 2), 2)
+        return wrap(z_at + far_first(i // 2), 8) * 2 + (x_high if i % 2 else 1 - x_high)
 
     def slot_of(y):
         q, b = y // 2, lax.rem(y, 2)
@@ -340,17 +362,18 @@
         return ref.at[(*where, pl.ds(pl.multiple_of(start, 8), size))]
 
     def ends(p, c, h, to):
-        half = 16 * lax.rem(x_low + 1 - h, 2)
+        half = 16 * (x_low if h else 1 - x_low)
         if p == 0:
             return send1.at[c, to], recv1.at[c, gx]
         if p == 1:
-            return at(send2, (c,), to * 16, 16), at(recv2, (c,), 256 * h + lax.rem(gx, 16) * 16, 16)
+            return at(send2, (c,), to * 16, 16), at(recv2, (c,), 256 * h + (gx - 16 * x_low) * 16, 16)
         if p == 2:
             return at(send3, (c,), 256 * h + slot_of(to) * 16, 16), at(recv3, (c,), gy * 32 + half, 16)
         if p == 3:
             return at(send4, (c,), to * 32 + half, 16), at(recv4, (c,), 256 * h + slot_of(gy) * 16, 16)
         if p == 4:
-            return at(send5, (c,), 256 * h + lax.rem(to, 16) * 16, 16), at(recv5, (c,), gx * 16, 16)
+            there = x_low if h else 1 - x_low
+            return at(send5, (c,), 256 * h + (to - 16 * there) * 16, 16), at(recv5, (c,), gx * 16, 16)
         return at(send6, (c,), to * 8, 8), recv6.at[pl.ds(pl.multiple_of(gx * 16 + 8 * c, 8), 8)]
 
     def message(p, c, h, i):
@@ -370,13 +393,10 @@
         return pltpu.make_async_copy(source, target, local_sem.at[p, c, h])
 
     def start(p, c, h):
-        def body(i, carry):
+        for i in range(count(p, h)):
             message(p, c, h, i).start()
-            return carry
-
         if count(p, h) == 15:
             own_copy(p, c, h).start()
-        lax.fori_loop(0, count(p, h), body, 0)
 
     def group(some, p, c, h):
         return pltpu.make_async_remote_copy(
@@ -421,8 +441,20 @@
             device_id_type=MESH,
         )
 
-    weights_first = relay(weights.at[pl.ds(8, 8)], weights_mid, 0, {"gy": NGY - 1 - gy})
-    weights_second = relay(weights_turned, weights_got, 1, {"gx": NGX - 1 - gx})
+    weights_first = relay(weights.at[pl.ds(8, 8)], weights_mid, 0, across)
+    weights_second = relay(weights_turned, weights_got, 1, {"gx": 32 * x_low + 15 - gx})
+
+    def first_pieces(begin, end):
+        for k in range(begin, end):
+            lanes = pl.ds(1024 * k, 1024)
+            relay(weights.at[pl.ds(8, 8), lanes], weights_mid.at[:, lanes], 0, across).start()
+
+    def second_pieces(begin, end):
+        for k in range(begin, end):
+            rows = pl.ds(64 * k, 64)
+            where = {"gx": 32 * x_low + 15 - gx}
+            relay(weights_turned.at[rows], weights_got.at[rows], 1, where).start()
+
     row_first = relay(row0_send, row0_mid, 2, {"gy": lax.rem(NGY - gy, NGY)})
     edge_gx = jnp.where(gx == 0, 16, jnp.where(gx == 16, 0, lax.rem(NGX - gx, NGX)))
     row_second = relay(row0_mid, row0_got, 3, {"gx": jnp.where(gy == 0, edge_gx, NGX - 1 - gx)})
@@ -431,7 +463,7 @@
     for c in range(2):
         for h in range(2):
             start(0, c, h)
-    weights_first.start()
+            first_pieces(4 * c + 2 * h, 4 * c + 2 * h + 2)
 
     @pl.when(row_moves)
     def _():
@@ -474,16 +506,16 @@
     order_ref = get("order")[0]
     weights_first.wait_recv()
 
-    @pl.when(lower)
+    @pl.when(jnp.logical_not(lower))
     def _():
         weights_mid[0:1, :] = jnp.zeros((1, N), F32)
         weights_turned[...] = mirror_layout(weights_mid[...], flip, order_ref[1])
 
-    @pl.when(jnp.logical_not(lower))
+    @pl.when(lower)
     def _():
         weights_turned[...] = mirror_layout(weights_mid[...], flip, order_ref[0])
 
-    weights_second.start()
+    second_pieces(0, 2)
 
     @pl.when(jnp.logical_not(lower))
     def _():
@@ -509,6 +541,7 @@
                 rows = slice(256 * h + 16 * slot, 256 * h + 16 * slot + 16)
                 send3[c, rows] = recv2[c, pl.ds(256 * h + slot, 16, stride=16), :]
             start(2, c, h)
+            second_pieces(2 + 2 * c + h, 8 if c + h == 2 else 3 + 2 * c + h)
 
     ready("c512", "s512", "twist_rows", "sixteen", "sixteen_back")
     c512, s512 = [r[...] for r in get("c512")], [r[...] for r in get("s512")]
@@ -621,9 +654,10 @@
         p_edge = jnp.broadcast_to(cols[:, 3:4], (32, 128))
         first_left = face_flux(r_edge, r[:, :128], p_edge, p[:, :128])[:, 0:1]
         left = jnp.where(lane == 0, first_left, pltpu.roll(right, 1, 1))
-        div_out[32 * block : 32 * block + 32, :] = (above - below) + (right - left)
-    div_store = pltpu.make_async_copy(div_out, div_ref, load_sem.at[3])
-    div_store.start()
+        change = TIME_STEP * ((above - below) + (right - left))
+        new_out[32 * block : 32 * block + 32, :] = 0.5 * (r - change)
+    new_store = pltpu.make_async_copy(new_out, new_ref, load_sem.at[3])
+    new_store.start()
 
     for p in range(6):
         for c in range(2):
@@ -644,11 +678,12 @@
         row_second.wait_send()
 
     pot_store.wait()
-    div_store.wait()
+    new_store.wait()
 
 
 def local(density, kernel_hat):
     constants, index = flat_constants()
+    pieces, packs = pack(constants)
     vmem = lambda *shape: pltpu.VMEM(shape, F32)
     dma = lambda *shape: pltpu.SemaphoreType.DMA(shape)
     n_const = len(constants)
@@ -661,21 +696,21 @@
         vmem(2, 256, 256), vmem(512, 256),
         vmem(4, 1, COLS), vmem(4, 1, ROWS), vmem(4, 1, COLS), vmem(4, 1, ROWS),
         vmem(ROWS + 16, COLS), vmem(ROWS + 16, COLS), vmem(ROWS, COLS), vmem(ROWS, COLS),
-        dma(6, 2), dma(6, 2, 2), dma(6, 2, 2), dma(4), dma(n_const), dma(4), dma(4), dma(8), dma(8),
+        dma(6, 2), dma(6, 2, 2), dma(6, 2, 2), dma(4), dma(len(pieces)), dma(4), dma(4), dma(8), dma(8),
     ]
     out = jax.ShapeDtypeStruct((ROWS, COLS), F32)
-    half_potential, divergence = pl.pallas_call(
-        functools.partial(kernel, index, n_const),
+    half_potential, half_density = pl.pallas_call(
+        functools.partial(kernel, index, n_const, pieces),
         out_shape=(out, out),
-        in_specs=[pl.BlockSpec(memory_space=pl.ANY)] * (2 + n_const),
+        in_specs=[pl.BlockSpec(memory_space=pl.ANY)] * 4,
         out_specs=(pl.BlockSpec(memory_space=pl.ANY),) * 2,
         scratch_shapes=scratch,
         compiler_params=pltpu.CompilerParams(
-            collective_id=0, has_side_effects=True, vmem_limit_bytes=56 * 1024 * 1024
+            collective_id=0, has_side_effects=True, vmem_limit_bytes=52 * 1024 * 1024
         ),
         name="convolve_step",
-    )(density, kernel_hat, *[jnp.asarray(c) for c in constants])
-    return 2.0 * half_potential, density - TIME_STEP * divergence
+    )(density, kernel_hat, *[jnp.asarray(p) for p in packs])
+    return 2.0 * half_potential, 2.0 * half_density
 
 
 def solution(mesh):

time: 108 us -> 102 us (0.944)
  Pallas kernels: 105 us -> 98.8 us
  other arithmetic: 2.33 us -> 1.06 us
    pallas_call x1, Pallas kernels: 105 us -> 98.8 us  [local(): pl.pallas_call(functools.partial(kernel, index, n_const, pieces), out_sha...]
    sub x1 -> x0, other arithmetic: 2.33 us -> none  [local(): return (2.0 * half_potential, density - TIME_STEP * divergence)]
where the time goes in v3:
time: 102 us
  Pallas kernels  98.8 us (97%)
  other arithmetic  1.06 us (1%)
  local copies, waits for them, and re-layouts  1.03 us (1%)
    pallas_call x1, Pallas kernels, local(): pl.pallas_call(functools.partial(kernel, index, n_const, pieces), out_sha...  98.8 us

profile of v3, /device:TPU:1, one launch (start us, length us, event | category | flops | bytes accessed | tf_op | source)
XLA Modules:
  0.0 101.5 jit_solution(16067899696404347565)
XLA Ops:
  0.6 0.0 copy-start
  0.6 1.0 %copy-done = f32[256,512]{1,0:T(8,128)S(1)} copy-done((f32[256,512]{1,0:T(8,128)S(1)}, f32[256,512]{1,0:T(8,128)}, u32[]{:S(2)}) %copy-start) | copy-done | bytes 524312
  1.7 98.8 %convolve_step.1 = (f32[256,512]{1,0:T(8,128)S(1)}, f32[256,512]{1,0:T(8,128)S(1)}) custom-call(f32[256,512]{1,0:T(8,128)S(1)} %copy-done, f32[16,8192]{1,0:T(8,128)} %refs_1_.1, f32[2560,1024]{1,0:T(8,128)} %constant.6.clone.refs_2_, bf16[8480,1024]{1,0:T(8,128)(2,1)} %constant.7.clone.refs_3_), custom_call_target="tpu_custom_call" | custom-call | tf_op jit(solution)/shard_map/convolve_step/pallas_call | solution.py:702
  100.5 1.1 %broadcast_multiply_fusion = (f32[256,512]{1,0:T(8,128)}, f32[256,512]{1,0:T(8,128)}) fusion(f32[256,512]{1,0:T(8,128)S(1)} %get-tuple-element.5, f32[256,512]{1,0:T(8,128)S(1)} %get-tuple-element.4), kind=kLoop, calls=%fused_computation | loop fusion | flops 262144 | bytes 2097152 | tf_op jit(solution)/shard_map/mul | solution.py:713
Async XLA Ops:
  0.6 1.0 %copy-start = (f32[256,512]{1,0:T(8,128)S(1)}, f32[256,512]{1,0:T(8,128)}, u32[]{:S(2)}) copy-start(f32[256,512]{1,0:T(8,128)} %refs_0_.1) | copy-start | bytes 1572868

commit v4 on v3

--- a/solution.py
+++ b/solution.py
@@ -501,47 +501,51 @@
         start(1, c, 0)
         start(1, c, 1)
 
-    ready("flip", "order")
-    flip = get("flip")[0][...]
-    order_ref = get("order")[0]
-    weights_first.wait_recv()
-
-    @pl.when(jnp.logical_not(lower))
-    def _():
-        weights_mid[0:1, :] = jnp.zeros((1, N), F32)
-        weights_turned[...] = mirror_layout(weights_mid[...], flip, order_ref[1])
-
-    @pl.when(lower)
-    def _():
-        weights_turned[...] = mirror_layout(weights_mid[...], flip, order_ref[0])
-
-    second_pieces(0, 2)
-
-    @pl.when(jnp.logical_not(lower))
-    def _():
-        row_second.wait_recv()
-        row = lax.broadcasted_iota(jnp.int32, (8, N), 0)
-
-        @pl.when(device == 256)
+    def relay_weights():
+        ready("flip", "order")
+        flip = get("flip")[0][...]
+        order_ref = get("order")[0]
+        weights_first.wait_recv()
+
+        @pl.when(jnp.logical_not(lower))
         def _():
-            one, two = weights[0:1, :], row0_got[...]
-            only[...] = jnp.where(row == 0, jnp.broadcast_to(0.5 * (two - one), (8, N)), 0.0)
-            change = direct_layout(only[...])
-            wk[...] = wk[...] + change
-            wk2[...] = change + mirror_layout(only[...], flip, order_ref[1])
-            row0_got[...] = 0.5 * (one + two)
-
-        only[...] = jnp.where(row == 0, jnp.broadcast_to(row0_got[...], (8, N)), 0.0)
-        wk[...] = wk[...] + mirror_layout(only[...], flip, order_ref[1])
-
-    for c in range(2):
+            weights_mid[0:1, :] = jnp.zeros((1, N), F32)
+            weights_turned[...] = mirror_layout(weights_mid[...], flip, order_ref[1])
+
+        @pl.when(lower)
+        def _():
+            weights_turned[...] = mirror_layout(weights_mid[...], flip, order_ref[0])
+
+        second_pieces(0, 4)
+
+        @pl.when(jnp.logical_not(lower))
+        def _():
+            row_second.wait_recv()
+            row = lax.broadcasted_iota(jnp.int32, (8, N), 0)
+
+            @pl.when(device == 256)
+            def _():
+                one, two = weights[0:1, :], row0_got[...]
+                only[...] = jnp.where(row == 0, jnp.broadcast_to(0.5 * (two - one), (8, N)), 0.0)
+                change = direct_layout(only[...])
+                wk[...] = wk[...] + change
+                wk2[...] = change + mirror_layout(only[...], flip, order_ref[1])
+                row0_got[...] = 0.5 * (one + two)
+
+            only[...] = jnp.where(row == 0, jnp.broadcast_to(row0_got[...], (8, N)), 0.0)
+            wk[...] = wk[...] + mirror_layout(only[...], flip, order_ref[1])
+
+    for c in range(2):
+        if c == 1:
+            relay_weights()
         for h in range(2):
             finish(1, c, h)
             for slot in range(16):
                 rows = slice(256 * h + 16 * slot, 256 * h + 16 * slot + 16)
                 send3[c, rows] = recv2[c, pl.ds(256 * h + slot, 16, stride=16), :]
             start(2, c, h)
-            second_pieces(2 + 2 * c + h, 8 if c + h == 2 else 3 + 2 * c + h)
+            if c == 1:
+                second_pieces(4 + 2 * h, 6 + 2 * h)
 
     ready("c512", "s512", "twist_rows", "sixteen", "sixteen_back")
     c512, s512 = [r[...] for r in get("c512")], [r[...] for r in get("s512")]

time: 102 us -> 103 us (level)
  Pallas kernels: 98.8 us -> 100 us
    pallas_call x1, Pallas kernels: 98.8 us -> 100 us  [local(): pl.pallas_call(functools.partial(kernel, index, n_const, pieces), out_sha...]
where the time goes in v4:
time: 103 us
  Pallas kernels  100 us (97%)
  other arithmetic  1.06 us (1%)
  local copies, waits for them, and re-layouts  1.03 us (1%)
    pallas_call x1, Pallas kernels, local(): pl.pallas_call(functools.partial(kernel, index, n_const, pieces), out_sha...  100 us

profile of v4, /device:TPU:1, one launch (start us, length us, event | category | flops | bytes accessed | tf_op | source)
XLA Modules:
  0.0 102.7 jit_solution(755778367293145707)
XLA Ops:
  0.6 0.0 copy-start
  0.6 1.0 %copy-done = f32[256,512]{1,0:T(8,128)S(1)} copy-done((f32[256,512]{1,0:T(8,128)S(1)}, f32[256,512]{1,0:T(8,128)}, u32[]{:S(2)}) %copy-start) | copy-done | bytes 524312
  1.7 100.0 %convolve_step.1 = (f32[256,512]{1,0:T(8,128)S(1)}, f32[256,512]{1,0:T(8,128)S(1)}) custom-call(f32[256,512]{1,0:T(8,128)S(1)} %copy-done, f32[16,8192]{1,0:T(8,128)} %refs_1_.1, f32[2560,1024]{1,0:T(8,128)} %constant.6.clone.refs_2_, bf16[8480,1024]{1,0:T(8,128)(2,1)} %constant.7.clone.refs_3_), custom_call_target="tpu_custom_call" | custom-call | tf_op jit(solution)/shard_map/convolve_step/pallas_call | solution.py:706
  101.6 1.1 %broadcast_multiply_fusion = (f32[256,512]{1,0:T(8,128)}, f32[256,512]{1,0:T(8,128)}) fusion(f32[256,512]{1,0:T(8,128)S(1)} %get-tuple-element.5, f32[256,512]{1,0:T(8,128)S(1)} %get-tuple-element.4), kind=kLoop, calls=%fused_computation | loop fusion | flops 262144 | bytes 2097152 | tf_op jit(solution)/shard_map/mul | solution.py:717
Async XLA Ops:
  0.6 1.0 %copy-start = (f32[256,512]{1,0:T(8,128)S(1)}, f32[256,512]{1,0:T(8,128)}, u32[]{:S(2)}) copy-start(f32[256,512]{1,0:T(8,128)} %refs_0_.1) | copy-start | bytes 1572868
